TPU v7x, 32 devices: a whole 2x2x4 slice. The times are simulated.
32 devices in a mesh: blk: 8 (over y, x, core), head: 4 (over z).
Axes of the slice: x: 2, y: 2, z: 4, core: 2. Of those that a mesh axis runs over, the one named last changes fastest.
Arguments:
- tokens: bfloat16 [4096, 768], P(('blk', 'head')), may hold values from -6 to 6
- w_qkv: bfloat16 [768, 2304], P('blk', 'head'), may hold values from -0.21875 to 0.21875
- w_out: bfloat16 [768, 768], P('head', 'blk'), may hold values from -0.875 to 0.875
- w_gate_up: bfloat16 [2, 768, 3072], P(None, 'blk', 'head'), may hold values from -0.21875 to 0.21875
- w_down: bfloat16 [3072, 768], P('head', 'blk'), may hold values from -0.109375 to 0.109375
- norm_params: bfloat16 [768, 4], P('blk', 'head'), may hold values from 0.25 to 1.75
- alibi_slope: float32 [12], replicated, may hold values from 0.00012207031 to 0.001953125
- lengths: int32 [8], replicated, may hold values from 1 to 2048, 4096 in all
- placement: int32 [4096], replicated, may hold values from 0 to 4095, as said below
- out_grad: bfloat16 [4096, 768], P(('blk', 'head')), may hold values from -6 to 6
Outputs:
- activations: bfloat16 [4096, 768], P(('blk', 'head'))
- input_grad: float32 [4096, 768], P(('blk', 'head'))
- grad_qkv: float32 [768, 2304], P('blk', 'head')
- grad_out: float32 [768, 768], P('head', 'blk')
- grad_gate_up: float32 [2, 768, 3072], P(None, 'blk', 'head')
- grad_down: float32 [3072, 768], P('head', 'blk')
- grad_norm: float32 [768, 4], P('blk', 'head')
Inputs may be any that keep to these rules, and one draw needn't show every extreme that they name: `placement`: A permutation of the positions: the row at slot s of a device's 128 rows holds a position from s * 32 to (s + 1) * 32 - 1, and each such run of positions has exactly one on every device.
All inputs are finite; a program needn't handle non-finite values.
Results may differ from a plain program's by a relative error of at most 0.023.
Values may be sent and summed in bfloat16 or wider, within the bound.
A program may use at most 128 MiB of HBM per device.

v0:
```python
import jax
import jax.numpy as jnp
from jax import lax
from jax.sharding import PartitionSpec as P

HEADS = 12
HEAD_DIM = 64


masked_score = -1e30


def layer_norm(residual, norm_gain, norm_shift):
    center = residual - jnp.mean(residual, axis=-1, keepdims=True)
    spread = jnp.mean(center * center, axis=-1, keepdims=True)
    return center * lax.rsqrt(spread + 1e-05) * norm_gain + norm_shift


def geglu(gate, upward):
    return jax.nn.gelu(gate, approximate=False) * upward


def dot_back(grad_rows, weight):
    return lax.dot_general(
        grad_rows, weight, (((1,), (1,)), ((), ())), preferred_element_type=jnp.float32
    )


def weight_grad(left, right):
    return lax.dot_general(
        left, right, (((0,), (0,)), ((), ())), preferred_element_type=jnp.float32
    )


def seq_of(positions, seq_ends):
    return jnp.sum((positions[:, None] >= seq_ends[None, :]).astype(jnp.int32), axis=1)


def biased_scores(queries, key_rows, q_pos, k_pos, q_seq, k_seq, slopes, qk_scale):
    scores = (
        jnp.einsum("qhd,khd->hqk", queries, key_rows, preferred_element_type=jnp.float32) * qk_scale
    )
    distance = jnp.abs(q_pos[:, None] - k_pos[None, :]).astype(jnp.float32)
    scores = scores - slopes[:, None, None] * distance[None]
    same_seq = (q_seq[:, None] == k_seq[None, :])[None]
    return (scores, same_seq)


def shards(
    tokens, w_qkv, w_out, w_gate_up, w_down, norm_params, alibi_slope, lengths, placement, out_grad
):
    heads_n = lax.axis_size("head")
    head_idx = lax.axis_index("head")
    blk_idx = lax.axis_index("blk")
    tok_rows = tokens.shape[0]
    per_dev = HEADS // heads_n
    group_rows = heads_n * tok_rows
    qk_scale = HEAD_DIM ** (-0.5)
    group_tokens, norm_cols = (
        lax.all_gather(tokens, "head", axis=0, tiled=True),
        lax.all_gather(norm_params, "head", axis=1, tiled=True),
    )
    f_qkv, f_out, f_gu, f_down, f_norm = (
        lax.all_gather(w_qkv, "blk", axis=0, tiled=True),
        lax.all_gather(w_out, "blk", axis=1, tiled=True),
        lax.all_gather(w_gate_up, "blk", axis=1, tiled=True),
        lax.all_gather(w_down, "blk", axis=1, tiled=True),
        lax.all_gather(norm_cols, "blk", axis=0, tiled=True),
    )
    grouped = jnp.dot(group_tokens, f_qkv, preferred_element_type=jnp.float32).astype(jnp.bfloat16)
    grouped = grouped.reshape(group_rows, per_dev, 3, HEAD_DIM)
    norms = f_norm.astype(jnp.float32)
    queries = grouped[:, :, 0]
    key_rows = grouped[:, :, 1]
    values = grouped[:, :, 2]
    seq_ends = jnp.cumsum(lengths)
    q_pos = lax.dynamic_slice_in_dim(placement, blk_idx * group_rows, group_rows)
    q_seq = seq_of(q_pos, seq_ends)
    slopes = lax.dynamic_slice_in_dim(alibi_slope, head_idx * per_dev, per_dev)

    def split_rows(shard_part):
        block_count = shard_part[0].shape[0] // group_rows
        pieces = tuple(
            (arr.reshape((block_count, group_rows) + arr.shape[1:]) for arr in shard_part)
        )
        starts = group_rows * jnp.arange(block_count, dtype=jnp.int32)
        return pieces + (starts,)

    start_state = (
        jnp.full((per_dev, group_rows), masked_score, jnp.float32),
        jnp.zeros((per_dev, group_rows), jnp.float32),
        jnp.zeros((group_rows, per_dev, HEAD_DIM), jnp.float32),
    )
    running = start_state

    def forward_per_block(state, block_in):
        k_blk, v_blk, k_first = block_in
        row_best, row_total, out_sum = state
        k_pos = lax.dynamic_slice_in_dim(placement, k_first, group_rows)
        scores, same_seq = biased_scores(
            queries, k_blk, q_pos, k_pos, q_seq, seq_of(k_pos, seq_ends), slopes, qk_scale
        )
        row_top = jnp.max(jnp.where(same_seq, scores, masked_score), axis=2)
        new_best = jnp.maximum(row_best, row_top)
        factor = jnp.exp(row_best - new_best)
        prob_tile = jnp.where(same_seq, jnp.exp(scores - new_best[:, :, None]), 0.0)
        row_total = row_total * factor + jnp.sum(prob_tile, axis=2)
        out_sum = out_sum * factor.T[:, :, None] + jnp.einsum(
            "hqk,khd->qhd",
            prob_tile.astype(jnp.bfloat16),
            v_blk,
            preferred_element_type=jnp.float32,
        )
        return ((new_best, row_total, out_sum), None)

    running, _ = lax.scan(
        forward_per_block,
        running,
        split_rows(
            (
                lax.all_gather(key_rows, "blk", axis=0, tiled=True),
                lax.all_gather(values, "blk", axis=0, tiled=True),
            )
        ),
    )
    row_best, row_total, out_sum = running
    attended = (out_sum / row_total.T[:, :, None]).astype(jnp.bfloat16)
    log_total = row_best + jnp.log(row_total)
    mixed = attended.reshape(group_rows, per_dev * HEAD_DIM)
    attn_out = lax.psum_scatter(
        jnp.dot(mixed, f_out, preferred_element_type=jnp.float32).astype(jnp.bfloat16),
        "head",
        scatter_dimension=0,
        tiled=True,
    ).astype(jnp.float32)
    resid_one = tokens.astype(jnp.float32) + attn_out
    hidden, norm_one_back = jax.vjp(layer_norm, resid_one, norms[:, 0], norms[:, 1])
    hidden_low = hidden.astype(jnp.bfloat16)
    ffn_rows = lax.all_gather(hidden_low, "head", axis=0, tiled=True)
    gate = jnp.dot(ffn_rows, f_gu[0], preferred_element_type=jnp.float32)
    upward = jnp.dot(ffn_rows, f_gu[1], preferred_element_type=jnp.float32)
    gated, geglu_back = jax.vjp(geglu, gate, upward)
    gated_low = gated.astype(jnp.bfloat16)
    branch_part = jnp.dot(gated_low, f_down, preferred_element_type=jnp.float32)
    branch = lax.psum_scatter(
        branch_part.astype(jnp.bfloat16), "head", scatter_dimension=0, tiled=True
    ).astype(jnp.float32)
    result, norm_two_back = jax.vjp(layer_norm, hidden + branch, norms[:, 2], norms[:, 3])
    d_two, d_gain_two, d_shift_two = norm_two_back(out_grad.astype(jnp.float32))
    d_branch = d_two.astype(jnp.bfloat16)
    branch_rows = lax.all_gather(d_branch, "head", axis=0, tiled=True)
    g_down = weight_grad(gated_low, branch_rows)
    d_gate, d_up = geglu_back(dot_back(branch_rows, f_down))
    d_gate_low = d_gate.astype(jnp.bfloat16)
    d_up_low = d_up.astype(jnp.bfloat16)
    g_gate_up = jnp.stack([weight_grad(ffn_rows, d_gate_low), weight_grad(ffn_rows, d_up_low)])
    hidden_part = dot_back(d_gate_low, f_gu[0]) + dot_back(d_up_low, f_gu[1])
    d_hidden = d_two + lax.psum_scatter(
        hidden_part.astype(jnp.bfloat16), "head", scatter_dimension=0, tiled=True
    ).astype(jnp.float32)
    d_one, d_gain_one, d_shift_one = norm_one_back(d_hidden)
    d_attn = d_one.astype(jnp.bfloat16)
    attn_rows = lax.all_gather(d_attn, "head", axis=0, tiled=True)
    g_out = weight_grad(mixed, attn_rows)
    d_heads = dot_back(attn_rows, f_out).astype(jnp.bfloat16).reshape(group_rows, per_dev, HEAD_DIM)
    delta = jnp.sum(d_heads.astype(jnp.float32) * attended.astype(jnp.float32), axis=2).T
    zero_grad = jnp.zeros((group_rows, per_dev, HEAD_DIM), jnp.float32)
    grad_q = zero_grad

    def query_per_block(running, block_in):
        k_blk, v_blk, k_first = block_in
        k_pos = lax.dynamic_slice_in_dim(placement, k_first, group_rows)
        scores, same_seq = biased_scores(
            queries, k_blk, q_pos, k_pos, q_seq, seq_of(k_pos, seq_ends), slopes, qk_scale
        )
        prob_tile = jnp.where(same_seq, jnp.exp(scores - log_total[:, :, None]), 0.0)
        d_prob = jnp.einsum("qhd,khd->hqk", d_heads, v_blk, preferred_element_type=jnp.float32)
        d_score = (prob_tile * (d_prob - delta[:, :, None])).astype(jnp.bfloat16)
        running = (
            running
            + jnp.einsum("hqk,khd->qhd", d_score, k_blk, preferred_element_type=jnp.float32)
            * qk_scale
        )
        return (running, None)

    grad_q, _ = lax.scan(
        query_per_block,
        grad_q,
        split_rows(
            (
                lax.all_gather(key_rows, "blk", axis=0, tiled=True),
                lax.all_gather(values, "blk", axis=0, tiled=True),
            )
        ),
    )
    stats_lse, stats_delta = (
        lax.all_gather(log_total, "blk", axis=1, tiled=True),
        lax.all_gather(delta, "blk", axis=1, tiled=True),
    )
    running = (zero_grad, zero_grad)

    def key_per_block(state, block_in):
        q_blk, do_blk, q_first = block_in
        grad_k, grad_v = state
        other_pos = lax.dynamic_slice_in_dim(placement, q_first, group_rows)
        lse_blk = lax.dynamic_slice_in_dim(stats_lse, q_first, group_rows, 1)
        delta_blk = lax.dynamic_slice_in_dim(stats_delta, q_first, group_rows, 1)
        scores, same_seq = biased_scores(
            q_blk, key_rows, other_pos, q_pos, seq_of(other_pos, seq_ends), q_seq, slopes, qk_scale
        )
        prob_tile = jnp.where(same_seq, jnp.exp(scores - lse_blk[:, :, None]), 0.0)
        grad_v = grad_v + jnp.einsum(
            "hqk,qhd->khd",
            prob_tile.astype(jnp.bfloat16),
            do_blk,
            preferred_element_type=jnp.float32,
        )
        d_prob = jnp.einsum("qhd,khd->hqk", do_blk, values, preferred_element_type=jnp.float32)
        d_score = (prob_tile * (d_prob - delta_blk[:, :, None])).astype(jnp.bfloat16)
        grad_k = (
            grad_k
            + jnp.einsum("hqk,qhd->khd", d_score, q_blk, preferred_element_type=jnp.float32)
            * qk_scale
        )
        return ((grad_k, grad_v), None)

    running, _ = lax.scan(
        key_per_block,
        running,
        split_rows(
            (
                lax.all_gather(queries, "blk", axis=0, tiled=True),
                lax.all_gather(d_heads, "blk", axis=0, tiled=True),
            )
        ),
    )
    grad_k, grad_v = running
    d_grouped = jnp.stack([grad_q, grad_k, grad_v], axis=2).astype(jnp.bfloat16)
    g_norm = jnp.stack([d_gain_one, d_shift_one, d_gain_two, d_shift_two], axis=1)
    d_qkv = d_grouped.reshape(group_rows, per_dev * 3 * HEAD_DIM)
    g_qkv = weight_grad(group_tokens, d_qkv)
    input_sum, norm_share = (
        lax.psum_scatter(
            dot_back(d_qkv, f_qkv).astype(jnp.bfloat16), "head", scatter_dimension=0, tiled=True
        ).astype(jnp.float32),
        lax.psum_scatter(
            g_norm.astype(jnp.bfloat16), "head", scatter_dimension=1, tiled=True
        ).astype(jnp.float32),
    )
    input_grad = d_one + input_sum
    s_qkv, s_out, s_gu, s_down, s_norm = (
        lax.psum_scatter(g_qkv, "blk", scatter_dimension=0, tiled=True),
        lax.psum_scatter(g_out, "blk", scatter_dimension=1, tiled=True),
        lax.psum_scatter(g_gate_up, "blk", scatter_dimension=1, tiled=True),
        lax.psum_scatter(g_down, "blk", scatter_dimension=1, tiled=True),
        lax.psum_scatter(norm_share, "blk", scatter_dimension=0, tiled=True),
    )
    return (result.astype(jnp.bfloat16), input_grad, s_qkv, s_out, s_gu, s_down, s_norm)


def solution(mesh):
    placed = (
        P(("blk", "head"), None),
        P("blk", "head"),
        P("head", "blk"),
        P(None, "blk", "head"),
        P("head", "blk"),
        P("blk", "head"),
        P(),
        P(),
        P(),
        P(("blk", "head"), None),
    )
    return jax.shard_map(
        shards,
        mesh=mesh,
        in_specs=placed,
        out_specs=(
            P(("blk", "head"), None),
            P(("blk", "head"), None),
            P("blk", "head"),
            P("head", "blk"),
            P(None, "blk", "head"),
            P("head", "blk"),
            P("blk", "head"),
        ),
        check_vma=False,
    )
```

profile of v0, /device:TPU:0, one launch (start us, length us, event | category | flops | bytes accessed | tf_op | source)
XLA Modules:
  0.0 834.2 jit_solution(2258512166681552994)
XLA Ops:
  7.2 12.6 %all_gather.51 = bf16[768,576]{1,0:T(8,128)(2,1)S(1)} all-gather(bf16[96,576]{1,0:T(8,128)(2,1)} %param.17), channel_id=1, replica_groups=mesh['blk'=8,'head'=4] {'blk'}, dimensions={0}, use_global_device_ids=true | all-gather | bytes 995328 | tf_op jit(solution)/shard_map/all_gather | solution.py:64
  19.8 20.0 %all_gather.50 = bf16[512,768]{1,0:T(8,128)(2,1)S(1)} all-gather(bf16[128,768]{1,0:T(8,128)(2,1)} %param.16), channel_id=1, replica_groups=mesh['blk'=8,'head'=4] {'head'}, dimensions={0}, use_global_device_ids=true | all-gather | bytes 983040 | tf_op jit(solution)/shard_map/all_gather | solution.py:60
  44.1 10.6 %all_gather.54 = bf16[192,768]{0,1:T(8,128)(2,1)} all-gather(bf16[192,96]{0,1:T(8,128)(2,1)S(1)} %copy.67), channel_id=1, replica_groups=mesh['blk'=8,'head'=4] {'blk'}, dimensions={1}, use_global_device_ids=true | all-gather | bytes 331776 | tf_op jit(solution)/shard_map/all_gather | solution.py:65
  55.9 10.7 %all-gather.18.cloned.1.call-done = bf16[4096,3,1,64]{0,3,2,1:T(8,128)(2,1)} async-done(((bf16[512,3,1,64]{0,3,2,1:T(8,128)(2,1)}), bf16[4096,3,1,64]{0,3,2,1:T(8,128)(2,1)}) %all-gather.18.cloned.1.call-update) | async-done | bytes 1572880 | tf_op jit(solution)/shard_map/all_gather | solution.py:121
  69.1 25.8 %all-gather.20.cloned.1.call-done = bf16[4096,3,1,64]{0,3,2,1:T(8,128)(2,1)} async-done(((bf16[512,3,1,64]{0,3,2,1:T(8,128)(2,1)}), bf16[4096,3,1,64]{0,3,2,1:T(8,128)(2,1)}) %all-gather.20.cloned.1.call-update) | async-done | bytes 1572880 | tf_op jit(solution)/shard_map/all_gather | solution.py:122
  98.7 102.2 %while.39 = (s32[]{:T(128)}, f32[3,512]{1,0:T(4,128)S(1)}, f32[3,512]{1,0:T(4,128)S(1)}, f32[512,3,64]{0,2,1:T(8,128)}, s32[512]{0:T(512)S(1)}, /*index=5*/s32[8...) while((s32[]{:T(128)}, f32[3,512]{1,0:T(4,128)S(1)}, ...), condition=%wide.region_6.7_spmd.clone, body=%wide.region_2.6_spmd.clone.sunk | while | flops 216060416 | bytes 28755240 | solution.py:116
  119.2 4.0 fusion.160
  132.0 4.0 fusion.160
  144.7 4.0 fusion.160
  157.5 4.0 fusion.160
  170.3 4.0 fusion.160
  183.1 4.0 fusion.160
  195.9 4.0 fusion.160
  206.1 10.9 %all-gather.3 = bf16[4,1,96]{2,1,0:T(2,128)(2,1)S(1)} all-gather(bf16[1,1,96]{2,1,0:T(2,128)(2,1)S(1)} %bitcast.275), channel_id=1, replica_groups=mesh['blk'=8,'head'=4] {'head'}, dimensions={0}, use_global_device_ids=true | all-gather | bytes 960 | tf_op jit(solution)/shard_map/all_gather | solution.py:61
  216.9 8.8 %all-gather.4 = bf16[8,96,4]{1,2,0:T(4,128)(2,1)S(1)} all-gather(bf16[1,96,4]{1,2,0:T(4,128)(2,1)S(1)} %bitcast.274), channel_id=1, replica_groups=mesh['blk'=8,'head'=4] {'blk'}, dimensions={0}, use_global_device_ids=true | all-gather | bytes 6912 | tf_op jit(solution)/shard_map/all_gather | solution.py:68
  231.6 18.1 %all_gather.57 = bf16[512,768]{1,0:T(8,128)(2,1)S(1)} all-gather(bf16[128,768]{1,0:T(8,128)(2,1)S(1)} %fusion.90), channel_id=1, replica_groups=mesh['blk'=8,'head'=4] {'head'}, dimensions={0}, use_global_device_ids=true | all-gather | bytes 983040 | tf_op jit(solution)/shard_map/all_gather | solution.py:139
  249.8 8.6 %all-gather.12.cloned.1.call-done = bf16[2,768,768]{2,1,0:T(8,128)(2,1)} async-done(((bf16[2,96,768]{2,1,0:T(8,128)(2,1)}), bf16[2,768,768]{2,1,0:T(8,128)(2,1)}) %all-gather.12.cloned.1.call-update) | async-done | bytes 2359312 | tf_op jit(solution)/shard_map/all_gather | solution.py:66
  261.8 5.2 multiply_convert_fusion.2
  267.1 17.1 %all-gather.14.cloned.1.call-done = bf16[768,768]{0,1:T(8,128)(2,1)} async-done(((bf16[768,96]{0,1:T(8,128)(2,1)}), bf16[768,768]{0,1:T(8,128)(2,1)}) %all-gather.14.cloned.1.call-update) | async-done | bytes 1179664 | tf_op jit(solution)/shard_map/all_gather | solution.py:67
  288.0 22.6 %reduce-scatter.18.cloned.1.call-done = bf16[128,768]{1,0:T(8,128)(2,1)} async-done(((bf16[512,768]{1,0:T(8,128)(2,1)}), bf16[128,768]{1,0:T(8,128)(2,1)}) %reduce-scatter.18.cloned.1.call-update) | async-done | bytes 196624 | tf_op jit(solution)/shard_map/reduce_scatter | solution.py:145
  314.0 18.0 %all_gather.60 = bf16[512,768]{1,0:T(8,128)(2,1)S(1)} all-gather(bf16[128,768]{1,0:T(8,128)(2,1)S(1)} %add_convert_fusion.4), channel_id=1, replica_groups=mesh['blk'=8,'head'=4] {'head'}, dimensions={0}, use_global_device_ids=true | all-gather | bytes 983040 | tf_op jit(solution)/shard_map/all_gather | solution.py:151
  343.2 10.1 %all_gather.63 = f32[3,4096]{1,0:T(4,128)} all-gather(f32[3,512]{1,0:T(4,128)S(1)} %log_add_fusion), channel_id=1, replica_groups=mesh['blk'=8,'head'=4] {'blk'}, dimensions={1}, use_global_device_ids=true | all-gather | bytes 55296 | tf_op jit(solution)/shard_map/all_gather | solution.py:197
  353.9 10.0 %reduce-scatter.20.cloned.1.call-done = bf16[128,768]{1,0:T(8,128)(2,1)} async-done(((bf16[512,768]{1,0:T(8,128)(2,1)}), bf16[128,768]{1,0:T(8,128)(2,1)}) %reduce-scatter.20.cloned.1.call-update) | async-done | bytes 196624 | tf_op jit(solution)/shard_map/reduce_scatter | solution.py:158
  367.2 18.1 %all_gather.61 = bf16[512,768]{1,0:T(8,128)(2,1)S(1)} all-gather(bf16[128,768]{1,0:T(8,128)(2,1)S(1)} %add_convert_fusion.3), channel_id=1, replica_groups=mesh['blk'=8,'head'=4] {'head'}, dimensions={0}, use_global_device_ids=true | all-gather | bytes 983040 | tf_op jit(solution)/shard_map/all_gather | solution.py:163
  387.7 100.5 %while.40 = (s32[]{:T(128)}, f32[512,3,64]{0,2,1:T(8,128)}, bf16[8,512,3,64]{1,3,2,0:T(8,128)(2,1)}, s32[512]{0:T(512)S(1)}, s32[8]{0:T(128)}, /*index=5*/s32[40...) while((s32[]{:T(128)}, f32[512,3,64]{0,2,1:T(8,128)}, ...), condition=%wide.region_21.22_spmd.clone, body=%wide.region_19.21_spmd.clone.sunk | while | flops 309636608 | bytes 10739989 | solution.py:186
  396.1 4.1 fusion.167
  408.5 4.2 fusion.167
  421.1 4.2 fusion.167
  433.7 4.2 fusion.167
  446.3 4.2 fusion.167
  458.8 4.2 fusion.167
  471.4 4.2 fusion.167
  484.0 4.2 fusion.167
  490.2 10.2 %all-reduce = bf16[768,4]{0,1:T(4,128)(2,1)S(1)} all-reduce(bf16[768,4]{0,1:T(4,128)(2,1)S(1)} %pad_maximum_fusion.2), channel_id=13, replica_groups=mesh['blk'=8,'head'=4] {'head'}, use_global_device_ids=true, to_apply=%region_34.35.clone | all-reduce | flops 3072 | bytes 12288
  505.4 10.2 %all_gather.65 = f32[3,4096]{1,0:T(4,128)} all-gather(f32[3,512]{1,0:T(4,128)S(1)} %copy-done.30), channel_id=1, replica_groups=mesh['blk'=8,'head'=4] {'blk'}, dimensions={1}, use_global_device_ids=true | all-gather | bytes 55296 | tf_op jit(solution)/shard_map/all_gather | solution.py:198
  518.4 137.4 %while.41 = (s32[]{:T(128)}, f32[512,3,64]{0,2,1:T(8,128)}, f32[512,3,64]{0,2,1:T(8,128)}, bf16[8,512,3,64]{1,3,2,0:T(8,128)(2,1)}, s32[8]{0:T(128)}, /*index=5*...) while((s32[]{:T(128)}, f32[512,3,64]{0,2,1:T(8,128)}, ...), condition=%wide.region_24.25_spmd.clone, body=%wide.region_22.24_spmd.clone.sunk | while | flops 415215104 | bytes 16188678 | solution.py:227
  531.4 4.0 fusion.176
  548.5 4.2 fusion.176
  565.8 4.1 fusion.176
  583.0 4.1 fusion.176
  600.1 4.1 fusion.176
  617.3 4.1 fusion.176
  634.5 4.1 fusion.176
  651.7 4.1 fusion.176
  673.5 6.2 reduce-scatter.22.cloned.1.call-done
  681.5 43.9 %reduce-scatter.26.cloned.1.call-done = f32[768,96]{0,1:T(8,128)} async-done(((f32[768,768]{0,1:T(8,128)}), f32[768,96]{0,1:T(8,128)}) %reduce-scatter.26.cloned.1.call-update) | async-done | bytes 294928 | tf_op jit(solution)/shard_map/reduce_scatter | solution.py:255
  725.4 44.5 %reduce-scatter.28.cloned.1.call-done = f32[96,576]{1,0:T(8,128)} async-done(((f32[768,576]{1,0:T(8,128)}), f32[96,576]{1,0:T(8,128)}) %reduce-scatter.28.cloned.1.call-update) | async-done | bytes 221200
  769.9 57.8 %reduce-scatter.24.cloned.1.call-done = f32[2,96,768]{2,1,0:T(8,128)} async-done(((f32[2,768,768]{2,1,0:T(8,128)}), f32[2,96,768]{2,1,0:T(8,128)}) %reduce-scatter.24.cloned.1.call-update) | async-done | bytes 589840 | tf_op jit(solution)/shard_map/reduce_scatter | solution.py:254
  (449 shorter events, 277.8 us)
Async XLA Ops:
  7.2 59.4 %all-gather.18.cloned.1.call-start = ((), (), s32[]{:S(2)}) async-start(), calls=%async_computation.18 | async-start | bytes 1769472 | tf_op jit(solution)/shard_map/all_gather | solution.py:121
  19.8 20.7 %copy-start.19 = (bf16[768,576]{1,0:T(8,128)(2,1)}, bf16[768,576]{1,0:T(8,128)(2,1)S(1)}, u32[]{:S(2)}) copy-start(bf16[768,576]{1,0:T(8,128)(2,1)S(1)} %all_gather.51) | copy-start | bytes 2654212
  41.5 53.4 %all-gather.20.cloned.1.call-start = ((), (), s32[]{:S(2)}) async-start(), calls=%async_computation.19 | async-start | bytes 1769472 | tf_op jit(solution)/shard_map/all_gather | solution.py:122
  42.3 186.1 %reduce-scatter.16.cloned.1.call-start = ((), (), s32[]{:S(2)}) async-start(), calls=%async_computation.9 | async-start | bytes 983040 | tf_op jit(solution)/shard_map/reduce_scatter | solution.py:130
  200.9 5.1 copy-start.5
  200.9 5.1 copy-start.23
  200.9 5.1 copy-start.44
  200.9 27.4 %copy-start.1 = (bf16[128,768]{1,0:T(8,128)(2,1)S(1)}, bf16[128,768]{1,0:T(8,128)(2,1)}, u32[]{:S(2)}) copy-start(bf16[128,768]{1,0:T(8,128)(2,1)} %param.16) | copy-start | bytes 589828
  202.4 28.1 %copy-start.16 = (bf16[512,3,64]{0,2,1:T(8,128)(2,1)}, bf16[512,3,64]{0,2,1:T(8,128)(2,1)S(1)}, u32[]{:S(2)}) copy-start(bf16[512,3,64]{0,2,1:T(8,128)(2,1)S(1)} %divide_convert_fusion) | copy-start | bytes 589828
  204.8 53.5 %all-gather.12.cloned.1.call-start = ((), (), s32[]{:S(2)}) async-start(), calls=%async_computation.10 | async-start | bytes 2654208 | tf_op jit(solution)/shard_map/all_gather | solution.py:66
  205.4 78.8 %all-gather.14.cloned.1.call-start = ((), (), s32[]{:S(2)}) async-start(), calls=%async_computation.11 | async-start | bytes 1327104 | tf_op jit(solution)/shard_map/all_gather | solution.py:67
  206.0 104.7 %reduce-scatter.18.cloned.1.call-start = ((), (), s32[]{:S(2)}) async-start(), calls=%async_computation.12 | async-start | bytes 983040 | tf_op jit(solution)/shard_map/reduce_scatter | solution.py:145
  225.9 84.8 %copy-start.26 = (f32[768]{0:T(1024)}, f32[768]{0:T(1024)S(1)}, u32[]{:S(2)}) copy-start(f32[768]{0:T(1024)S(1)} %get-tuple-element.605) | copy-start | bytes 9220
  229.4 81.3 %copy-start.32 = (f32[128]{0:T(128)}, f32[128]{0:T(128)S(1)}, u32[]{:S(2)}) copy-start(f32[128]{0:T(128)S(1)} %broadcast_multiply_fusion.1) | copy-start | bytes 1540
  230.5 30.0 %copy-start.42 = (f32[128]{0:T(128)}, f32[128]{0:T(128)S(1)}, u32[]{:S(2)}) copy-start(f32[128]{0:T(128)S(1)} %multiply_reduce_fusion.4) | copy-start | bytes 1540
  230.6 80.1 %copy-start.35 = (f32[128]{0:T(128)}, f32[128]{0:T(128)S(1)}, u32[]{:S(2)}) copy-start(f32[128]{0:T(128)S(1)} %fusion.91) | copy-start | bytes 1540
  249.8 10.8 %copy-start.21 = (bf16[512,768]{1,0:T(8,128)(2,1)}, bf16[512,768]{1,0:T(8,128)(2,1)S(1)}, u32[]{:S(2)}) copy-start(bf16[512,768]{1,0:T(8,128)(2,1)S(1)} %all_gather.57) | copy-start | bytes 2359300
  267.1 20.1 %copy-start.13 = (bf16[512,768]{1,0:T(8,128)(2,1)}, bf16[512,768]{1,0:T(8,128)(2,1)S(1)}, u32[]{:S(2)}) copy-start(bf16[512,768]{1,0:T(8,128)(2,1)S(1)} %get-tuple-element.698) | copy-start | bytes 2359300
  284.2 26.5 %copy-start.4 = (bf16[128,768]{1,0:T(8,128)(2,1)S(1)}, bf16[128,768]{1,0:T(8,128)(2,1)}, u32[]{:S(2)}) copy-start(bf16[128,768]{1,0:T(8,128)(2,1)} %reduce-scatter.16.cloned.1.call-done) | copy-start | bytes 589828
  287.2 25.0 %copy-start.15 = (bf16[128,768]{1,0:T(8,128)(2,1)S(1)}, bf16[128,768]{1,0:T(8,128)(2,1)}, u32[]{:S(2)}) copy-start(bf16[128,768]{1,0:T(8,128)(2,1)} %param.25) | copy-start | bytes 589828
  287.2 52.2 %all-gather.22.cloned.1.call-start = ((), (), s32[]{:S(2)}) async-start(), calls=%async_computation.20 | async-start | bytes 1769472 | tf_op jit(solution)/shard_map/all_gather | solution.py:232
  288.0 76.0 %reduce-scatter.20.cloned.1.call-start = ((), (), s32[]{:S(2)}) async-start(), calls=%async_computation.13 | async-start | bytes 983040 | tf_op jit(solution)/shard_map/reduce_scatter | solution.py:158
  310.7 21.3 %copy-start.57 = (f32[512,768]{1,0:T(8,128)S(1)}, f32[512,768]{1,0:T(8,128)}, u32[]{:S(2)}) copy-start(f32[512,768]{1,0:T(8,128)} %get-tuple-element.699) | copy-start | bytes 4718596
  312.2 19.8 %copy-start.47 = (bf16[768,768]{0,1:T(8,128)(2,1)S(1)}, bf16[768,768]{0,1:T(8,128)(2,1)}, u32[]{:S(2)}) copy-start(bf16[768,768]{0,1:T(8,128)(2,1)} %all-gather.14.cloned.1.call-done) | copy-start | bytes 3538948
  312.2 19.8 %copy-start.52 = (f32[512,768]{1,0:T(8,128)S(1)}, f32[512,768]{1,0:T(8,128)}, u32[]{:S(2)}) copy-start(f32[512,768]{1,0:T(8,128)} %copy-done.51) | copy-start | bytes 4718596
  313.9 21.2 %copy-start.38 = (f32[128]{0:T(128)}, f32[128]{0:T(128)S(1)}, u32[]{:S(2)}) copy-start(f32[128]{0:T(128)S(1)} %negate_multiply_fusion.2) | copy-start | bytes 1540
  338.1 177.6 %all-gather.16.cloned.1.call-start = ((), (), s32[]{:S(2)}) async-start(), calls=%async_computation.14 | async-start | bytes 1769472 | tf_op jit(solution)/shard_map/all_gather | solution.py:233
  341.5 11.9 %copy-start.37 = (bf16[768]{0:T(1024)(128)(2,1)S(1)}, bf16[768]{0:T(1024)(128)(2,1)}, u32[]{:S(2)}) copy-start(bf16[768]{0:T(1024)(128)(2,1)} %get-tuple-element.600) | copy-start | bytes 4612
  341.5 22.5 %copy-start.27 = (f32[768]{0:T(1024)S(1)}, f32[768]{0:T(1024)}, u32[]{:S(2)}) copy-start(f32[768]{0:T(1024)} %copy-done.26) | copy-start | bytes 9220
  341.5 22.5 %copy-start.33 = (f32[128]{0:T(128)S(1)}, f32[128]{0:T(128)}, u32[]{:S(2)}) copy-start(f32[128]{0:T(128)} %copy-done.32) | copy-start | bytes 1540
  341.5 22.5 %copy-start.36 = (f32[128]{0:T(128)S(1)}, f32[128]{0:T(128)}, u32[]{:S(2)}) copy-start(f32[128]{0:T(128)} %copy-done.35) | copy-start | bytes 1540
  341.5 22.4 %copy-start.39 = (f32[128]{0:T(128)S(1)}, f32[128]{0:T(128)}, u32[]{:S(2)}) copy-start(f32[128]{0:T(128)} %copy-done.38) | copy-start | bytes 1540
  341.5 24.3 %copy-start.43 = (f32[128]{0:T(128)S(1)}, f32[128]{0:T(128)}, u32[]{:S(2)}) copy-start(f32[128]{0:T(128)} %copy-done.42) | copy-start | bytes 1540
  343.2 22.6 %copy-start.31 = (f32[3,512]{1,0:T(4,128)}, f32[3,512]{1,0:T(4,128)S(1)}, u32[]{:S(2)}) copy-start(f32[3,512]{1,0:T(4,128)S(1)} %log_add_fusion) | copy-start | bytes 18436
  365.8 20.5 %copy-start.8 = (bf16[192,768]{0,1:T(8,128)(2,1)S(1)}, bf16[192,768]{0,1:T(8,128)(2,1)}, u32[]{:S(2)}) copy-start(bf16[192,768]{0,1:T(8,128)(2,1)} %all_gather.54) | copy-start | bytes 884740
  367.1 20.3 %copy-start.6 = (f32[128,768]{1,0:T(8,128)}, f32[128,768]{1,0:T(8,128)S(1)}, u32[]{:S(2)}) copy-start(f32[128,768]{1,0:T(8,128)S(1)} %get-tuple-element.693) | copy-start | bytes 1179652
  367.1 19.6 %copy-start.18 = (f32[512,3,64]{0,2,1:T(8,128)S(1)}, f32[512,3,64]{0,2,1:T(8,128)}, u32[]{:S(2)}) copy-start(f32[512,3,64]{0,2,1:T(8,128)} %get-tuple-element.226) | copy-start | bytes 1179652
  367.1 19.6 %copy-start.25 = (f32[3,512]{1,0:T(4,128)S(1)}, f32[3,512]{1,0:T(4,128)}, u32[]{:S(2)}) copy-start(f32[3,512]{1,0:T(4,128)} %copy-done.23) | copy-start | bytes 18436
  367.1 20.3 %copy-start.40 = (f32[128]{0:T(128)}, f32[128]{0:T(128)S(1)}, u32[]{:S(2)}) copy-start(f32[128]{0:T(128)S(1)} %negate_multiply_fusion.1) | copy-start | bytes 1540
  387.4 283.0 %reduce-scatter.32.cloned.1.call-start = ((), (), s32[]{:S(2)}) async-start(), calls=%async_computation.23 | async-start | bytes 442368
  488.2 14.9 %copy-start.3 = (bf16[512,768]{1,0:T(8,128)(2,1)S(1)}, bf16[512,768]{1,0:T(8,128)(2,1)}, u32[]{:S(2)}) copy-start(bf16[512,768]{1,0:T(8,128)(2,1)} %copy-done.2) | copy-start | bytes 2359300
  505.3 166.5 %reduce-scatter.30.cloned.1.call-start = ((), (), s32[]{:S(2)}) async-start(), calls=%async_computation.22 | async-start | bytes 884736
  515.6 164.1 %reduce-scatter.22.cloned.1.call-start = ((), (), s32[]{:S(2)}) async-start(), calls=%async_computation.15 | async-start | bytes 983040 | tf_op jit(solution)/shard_map/reduce_scatter | solution.py:243
  659.0 66.5 %reduce-scatter.26.cloned.1.call-start = ((), (), s32[]{:S(2)}) async-start(), calls=%async_computation.17 | async-start | bytes 2654208 | tf_op jit(solution)/shard_map/reduce_scatter | solution.py:255
  661.3 108.6 %reduce-scatter.28.cloned.1.call-start = ((), (), s32[]{:S(2)}) async-start(), calls=%async_computation.21 | async-start | bytes 2211840
  665.0 162.7 %reduce-scatter.24.cloned.1.call-start = ((), (), s32[]{:S(2)}) async-start(), calls=%async_computation.16 | async-start | bytes 5308416 | tf_op jit(solution)/shard_map/reduce_scatter | solution.py:254
  670.4 9.3 %copy-start.7 = (f32[128,768]{1,0:T(8,128)S(1)}, f32[128,768]{1,0:T(8,128)}, u32[]{:S(2)}) copy-start(f32[128,768]{1,0:T(8,128)} %copy-done.6) | copy-start | bytes 1179652
  670.4 9.3 %copy-start.41 = (f32[128]{0:T(128)S(1)}, f32[128]{0:T(128)}, u32[]{:S(2)}) copy-start(f32[128]{0:T(128)} %copy-done.40) | copy-start | bytes 1540
  (39 other events, 93.2 us)
Sparse Core Ops, SparseCore 0:
  41.6 24.8 all-gather.17
  69.0 25.8 all-gather.19
  205.0 23.3 reduce-scatter.15
  230.1 28.2 all-gather.11
  260.1 24.0 all-gather.13
  287.4 23.2 reduce-scatter.17
  313.1 25.1 all-gather.21
  340.6 23.2 reduce-scatter.19
  387.5 25.1 all-gather.15
  505.5 31.9 reduce-scatter.31
  540.6 35.0 reduce-scatter.29
  659.1 20.5 reduce-scatter.21
  683.6 41.7 reduce-scatter.25
  729.6 40.2 reduce-scatter.27
  773.8 53.8 reduce-scatter.23
where the time goes:
time: 839 us; the launch traced here: 834 us
  waiting for transfers between devices  252 us (30%)
  matrix products  199 us (24%)
  blocking collectives  148 us (18%)
  local copies, waits for them, and re-layouts  86.4 us (10%)
  other arithmetic  86.1 us (10%)
  loops' own time  47.4 us (6%)
  between operations  14.7 us (2%)
    reduce_scatter x1, waiting for transfers between devices, shards(): lax.psum_scatter(g_gate_up, 'blk', scatter_dimension=1, tiled=True)  57.8 us
    unnamed x18, waiting for transfers between devices  47.2 us
    dot_general x24, matrix products, biased_scores(): jnp.einsum('qhd,khd->hqk', queries, key_rows, preferred_element_type=jnp....  45.9 us
    reduce_scatter x1, waiting for transfers between devices, shards(): lax.psum_scatter(g_down, 'blk', scatter_dimension=1, tiled=True)  43.9 us
    dot_general x8, matrix products, query_per_block(): jnp.einsum('hqk,khd->qhd', d_score, k_blk, preferred_element_type=jnp.flo...  33.5 us
    dot_general x8, matrix products, key_per_block(): jnp.einsum('hqk,qhd->khd', d_score, q_blk, preferred_element_type=jnp.flo...  32.7 us
    dot_general x8, matrix products, forward_per_block(): jnp.einsum('hqk,khd->qhd', prob_tile.astype(jnp.bfloat16), v_blk, preferr...  31.9 us
    dynamic_slice x24, local copies, waits for them, and re-layouts, shards(): lax.scan(forward_per_block, running, split_rows((lax.all_gather(key_rows,...  27.7 us
  transfers between devices with their start and end apart: 15, of which 11 were waited for; matrix products, arithmetic and copies ran while one was open for 32% of the time, Pallas kernels for 0%

commit v1 on v0

--- a/solution.py
+++ b/solution.py
@@ -34,6 +34,12 @@
 
 def seq_of(positions, seq_ends):
     return jnp.sum((positions[:, None] >= seq_ends[None, :]).astype(jnp.int32), axis=1)
+
+
+def prefix_sums(lengths):
+    count = lengths.shape[0]
+    upto = jnp.arange(count)[None, :] <= jnp.arange(count)[:, None]
+    return jnp.sum(jnp.where(upto, lengths[None, :], 0), axis=1)
 
 
 def biased_scores(queries, key_rows, q_pos, k_pos, q_seq, k_seq, slopes, qk_scale):
@@ -73,7 +79,7 @@
     queries = grouped[:, :, 0]
     key_rows = grouped[:, :, 1]
     values = grouped[:, :, 2]
-    seq_ends = jnp.cumsum(lengths)
+    seq_ends = prefix_sums(lengths)
     q_pos = lax.dynamic_slice_in_dim(placement, blk_idx * group_rows, group_rows)
     q_seq = seq_of(q_pos, seq_ends)
     slopes = lax.dynamic_slice_in_dim(alibi_slope, head_idx * per_dev, per_dev)

time: 839 us -> 839 us (level)
  no operation moved by 1% of the time
where the time goes in v1:
time: 839 us; the launch traced here: 834 us
  waiting for transfers between devices  252 us (30%)
  matrix products  199 us (24%)
  blocking collectives  148 us (18%)
  local copies, waits for them, and re-layouts  86.4 us (10%)
  other arithmetic  86.1 us (10%)
  loops' own time  47.4 us (6%)
  between operations  14.7 us (2%)
    reduce_scatter x1, waiting for transfers between devices, shards(): lax.psum_scatter(g_gate_up, 'blk', scatter_dimension=1, tiled=True)  57.8 us
    unnamed x18, waiting for transfers between devices  47.2 us
    dot_general x24, matrix products, biased_scores(): jnp.einsum('qhd,khd->hqk', queries, key_rows, preferred_element_type=jnp....  45.9 us
    reduce_scatter x1, waiting for transfers between devices, shards(): lax.psum_scatter(g_down, 'blk', scatter_dimension=1, tiled=True)  44 us
    dot_general x8, matrix products, query_per_block(): jnp.einsum('hqk,khd->qhd', d_score, k_blk, preferred_element_type=jnp.flo...  33.5 us
    dot_general x8, matrix products, key_per_block(): jnp.einsum('hqk,qhd->khd', d_score, q_blk, preferred_element_type=jnp.flo...  32.7 us
    dot_general x8, matrix products, forward_per_block(): jnp.einsum('hqk,khd->qhd', prob_tile.astype(jnp.bfloat16), v_blk, preferr...  31.9 us
    dynamic_slice x24, local copies, waits for them, and re-layouts, shards(): lax.scan(forward_per_block, running, split_rows((lax.all_gather(key_rows,...  27.7 us
  transfers between devices with their start and end apart: 15, of which 11 were waited for; matrix products, arithmetic and copies ran while one was open for 32% of the time, Pallas kernels for 0%

profile of v1, /device:TPU:0, one launch (start us, length us, event | category | flops | bytes accessed | tf_op | source)
XLA Modules:
  0.0 834.1 jit_solution(6940530319056521301)
XLA Ops:
  7.2 12.6 %all_gather.51 = bf16[768,576]{1,0:T(8,128)(2,1)S(1)} all-gather(bf16[96,576]{1,0:T(8,128)(2,1)} %param.17), channel_id=1, replica_groups=mesh['blk'=8,'head'=4] {'blk'}, dimensions={0}, use_global_device_ids=true | all-gather | bytes 995328 | tf_op jit(solution)/shard_map/all_gather | solution.py:70
  19.8 20.0 %all_gather.50 = bf16[512,768]{1,0:T(8,128)(2,1)S(1)} all-gather(bf16[128,768]{1,0:T(8,128)(2,1)} %param.16), channel_id=1, replica_groups=mesh['blk'=8,'head'=4] {'head'}, dimensions={0}, use_global_device_ids=true | all-gather | bytes 983040 | tf_op jit(solution)/shard_map/all_gather | solution.py:66
  43.3 10.9 %all_gather.54 = bf16[192,768]{0,1:T(8,128)(2,1)} all-gather(bf16[192,96]{0,1:T(8,128)(2,1)S(1)} %copy.67), channel_id=1, replica_groups=mesh['blk'=8,'head'=4] {'blk'}, dimensions={1}, use_global_device_ids=true | all-gather | bytes 331776 | tf_op jit(solution)/shard_map/all_gather | solution.py:71
  56.1 10.3 %all-gather.18.cloned.1.call-done = bf16[4096,3,1,64]{0,3,2,1:T(8,128)(2,1)} async-done(((bf16[512,3,1,64]{0,3,2,1:T(8,128)(2,1)}), bf16[4096,3,1,64]{0,3,2,1:T(8,128)(2,1)}) %all-gather.18.cloned.1.call-update) | async-done | bytes 1572880 | tf_op jit(solution)/shard_map/all_gather | solution.py:127
  69.0 25.8 %all-gather.20.cloned.1.call-done = bf16[4096,3,1,64]{0,3,2,1:T(8,128)(2,1)} async-done(((bf16[512,3,1,64]{0,3,2,1:T(8,128)(2,1)}), bf16[4096,3,1,64]{0,3,2,1:T(8,128)(2,1)}) %all-gather.20.cloned.1.call-update) | async-done | bytes 1572880 | tf_op jit(solution)/shard_map/all_gather | solution.py:128
  98.5 102.2 %while.39 = (s32[]{:T(128)}, f32[3,512]{1,0:T(4,128)S(1)}, f32[3,512]{1,0:T(4,128)S(1)}, f32[512,3,64]{0,2,1:T(8,128)}, s32[512]{0:T(512)S(1)}, /*index=5*/s32[8...) while((s32[]{:T(128)}, f32[3,512]{1,0:T(4,128)S(1)}, ...), condition=%wide.region_6.7_spmd.clone, body=%wide.region_2.6_spmd.clone.sunk | while | flops 216060416 | bytes 28755240 | solution.py:122
  119.0 4.0 fusion.160
  131.8 4.0 fusion.160
  144.6 4.0 fusion.160
  157.4 4.0 fusion.160
  170.2 4.0 fusion.160
  183.0 4.0 fusion.160
  195.7 4.0 fusion.160
  205.9 10.8 %all-gather.3 = bf16[4,1,96]{2,1,0:T(2,128)(2,1)S(1)} all-gather(bf16[1,1,96]{2,1,0:T(2,128)(2,1)S(1)} %bitcast.273), channel_id=1, replica_groups=mesh['blk'=8,'head'=4] {'head'}, dimensions={0}, use_global_device_ids=true | all-gather | bytes 960 | tf_op jit(solution)/shard_map/all_gather | solution.py:67
  216.8 8.8 %all-gather.4 = bf16[8,96,4]{1,2,0:T(4,128)(2,1)S(1)} all-gather(bf16[1,96,4]{1,2,0:T(4,128)(2,1)S(1)} %bitcast.272), channel_id=1, replica_groups=mesh['blk'=8,'head'=4] {'blk'}, dimensions={0}, use_global_device_ids=true | all-gather | bytes 6912 | tf_op jit(solution)/shard_map/all_gather | solution.py:74
  231.5 18.1 %all_gather.57 = bf16[512,768]{1,0:T(8,128)(2,1)S(1)} all-gather(bf16[128,768]{1,0:T(8,128)(2,1)S(1)} %fusion.90), channel_id=1, replica_groups=mesh['blk'=8,'head'=4] {'head'}, dimensions={0}, use_global_device_ids=true | all-gather | bytes 983040 | tf_op jit(solution)/shard_map/all_gather | solution.py:145
  249.6 8.6 %all-gather.12.cloned.1.call-done = bf16[2,768,768]{2,1,0:T(8,128)(2,1)} async-done(((bf16[2,96,768]{2,1,0:T(8,128)(2,1)}), bf16[2,768,768]{2,1,0:T(8,128)(2,1)}) %all-gather.12.cloned.1.call-update) | async-done | bytes 2359312 | tf_op jit(solution)/shard_map/all_gather | solution.py:72
  261.7 5.2 multiply_convert_fusion.2
  266.9 17.1 %all-gather.14.cloned.1.call-done = bf16[768,768]{0,1:T(8,128)(2,1)} async-done(((bf16[768,96]{0,1:T(8,128)(2,1)}), bf16[768,768]{0,1:T(8,128)(2,1)}) %all-gather.14.cloned.1.call-update) | async-done | bytes 1179664 | tf_op jit(solution)/shard_map/all_gather | solution.py:73
  287.9 22.6 %reduce-scatter.18.cloned.1.call-done = bf16[128,768]{1,0:T(8,128)(2,1)} async-done(((bf16[512,768]{1,0:T(8,128)(2,1)}), bf16[128,768]{1,0:T(8,128)(2,1)}) %reduce-scatter.18.cloned.1.call-update) | async-done | bytes 196624 | tf_op jit(solution)/shard_map/reduce_scatter | solution.py:151
  313.9 18.0 %all_gather.60 = bf16[512,768]{1,0:T(8,128)(2,1)S(1)} all-gather(bf16[128,768]{1,0:T(8,128)(2,1)S(1)} %add_convert_fusion.4), channel_id=1, replica_groups=mesh['blk'=8,'head'=4] {'head'}, dimensions={0}, use_global_device_ids=true | all-gather | bytes 983040 | tf_op jit(solution)/shard_map/all_gather | solution.py:157
  343.1 10.1 %all_gather.63 = f32[3,4096]{1,0:T(4,128)} all-gather(f32[3,512]{1,0:T(4,128)S(1)} %log_add_fusion), channel_id=1, replica_groups=mesh['blk'=8,'head'=4] {'blk'}, dimensions={1}, use_global_device_ids=true | all-gather | bytes 55296 | tf_op jit(solution)/shard_map/all_gather | solution.py:203
  353.8 10.0 %reduce-scatter.20.cloned.1.call-done = bf16[128,768]{1,0:T(8,128)(2,1)} async-done(((bf16[512,768]{1,0:T(8,128)(2,1)}), bf16[128,768]{1,0:T(8,128)(2,1)}) %reduce-scatter.20.cloned.1.call-update) | async-done | bytes 196624 | tf_op jit(solution)/shard_map/reduce_scatter | solution.py:164
  367.1 18.1 %all_gather.61 = bf16[512,768]{1,0:T(8,128)(2,1)S(1)} all-gather(bf16[128,768]{1,0:T(8,128)(2,1)S(1)} %add_convert_fusion.3), channel_id=1, replica_groups=mesh['blk'=8,'head'=4] {'head'}, dimensions={0}, use_global_device_ids=true | all-gather | bytes 983040 | tf_op jit(solution)/shard_map/all_gather | solution.py:169
  387.5 100.5 %while.40 = (s32[]{:T(128)}, f32[512,3,64]{0,2,1:T(8,128)}, bf16[8,512,3,64]{1,3,2,0:T(8,128)(2,1)}, s32[512]{0:T(512)S(1)}, s32[8]{0:T(128)}, /*index=5*/s32[40...) while((s32[]{:T(128)}, f32[512,3,64]{0,2,1:T(8,128)}, ...), condition=%wide.region_21.22_spmd.clone, body=%wide.region_19.21_spmd.clone.sunk | while | flops 309636608 | bytes 10739989 | solution.py:192
  395.9 4.1 fusion.167
  408.4 4.2 fusion.167
  421.0 4.2 fusion.167
  433.5 4.2 fusion.167
  446.1 4.2 fusion.167
  458.7 4.2 fusion.167
  471.2 4.2 fusion.167
  483.8 4.2 fusion.167
  490.1 10.2 %all-reduce = bf16[768,4]{0,1:T(4,128)(2,1)S(1)} all-reduce(bf16[768,4]{0,1:T(4,128)(2,1)S(1)} %pad_maximum_fusion.2), channel_id=13, replica_groups=mesh['blk'=8,'head'=4] {'head'}, use_global_device_ids=true, to_apply=%region_34.35.clone | all-reduce | flops 3072 | bytes 12288
  505.2 10.2 %all_gather.65 = f32[3,4096]{1,0:T(4,128)} all-gather(f32[3,512]{1,0:T(4,128)S(1)} %copy-done.30), channel_id=1, replica_groups=mesh['blk'=8,'head'=4] {'blk'}, dimensions={1}, use_global_device_ids=true | all-gather | bytes 55296 | tf_op jit(solution)/shard_map/all_gather | solution.py:204
  518.3 137.4 %while.41 = (s32[]{:T(128)}, f32[512,3,64]{0,2,1:T(8,128)}, f32[512,3,64]{0,2,1:T(8,128)}, bf16[8,512,3,64]{1,3,2,0:T(8,128)(2,1)}, s32[8]{0:T(128)}, /*index=5*...) while((s32[]{:T(128)}, f32[512,3,64]{0,2,1:T(8,128)}, ...), condition=%wide.region_24.25_spmd.clone, body=%wide.region_22.24_spmd.clone.sunk | while | flops 415215104 | bytes 16188678 | solution.py:233
  531.2 4.0 fusion.176
  548.4 4.2 fusion.176
  565.6 4.1 fusion.176
  582.8 4.1 fusion.176
  600.0 4.1 fusion.176
  617.2 4.1 fusion.176
  634.4 4.1 fusion.176
  651.5 4.1 fusion.176
  673.4 6.1 reduce-scatter.22.cloned.1.call-done
  681.3 44.0 %reduce-scatter.26.cloned.1.call-done = f32[768,96]{0,1:T(8,128)} async-done(((f32[768,768]{0,1:T(8,128)}), f32[768,96]{0,1:T(8,128)}) %reduce-scatter.26.cloned.1.call-update) | async-done | bytes 294928 | tf_op jit(solution)/shard_map/reduce_scatter | solution.py:261
  725.2 44.5 %reduce-scatter.28.cloned.1.call-done = f32[96,576]{1,0:T(8,128)} async-done(((f32[768,576]{1,0:T(8,128)}), f32[96,576]{1,0:T(8,128)}) %reduce-scatter.28.cloned.1.call-update) | async-done | bytes 221200
  769.8 57.8 %reduce-scatter.24.cloned.1.call-done = f32[2,96,768]{2,1,0:T(8,128)} async-done(((f32[2,768,768]{2,1,0:T(8,128)}), f32[2,96,768]{2,1,0:T(8,128)}) %reduce-scatter.24.cloned.1.call-update) | async-done | bytes 589840 | tf_op jit(solution)/shard_map/reduce_scatter | solution.py:260
  (449 shorter events, 277.8 us)
Async XLA Ops:
  7.2 59.3 %all-gather.18.cloned.1.call-start = ((), (), s32[]{:S(2)}) async-start(), calls=%async_computation.18 | async-start | bytes 1769472 | tf_op jit(solution)/shard_map/all_gather | solution.py:127
  19.8 20.7 %copy-start.19 = (bf16[768,576]{1,0:T(8,128)(2,1)}, bf16[768,576]{1,0:T(8,128)(2,1)S(1)}, u32[]{:S(2)}) copy-start(bf16[768,576]{1,0:T(8,128)(2,1)S(1)} %all_gather.51) | copy-start | bytes 2654212
  40.6 14.1 %copy-start.49 = (s32[8]{0:T(128)S(1)}, s32[8]{0:T(128)}, u32[]{:S(2)}) copy-start(s32[8]{0:T(128)} %param.23) | copy-start | bytes 100
  41.5 53.3 %all-gather.20.cloned.1.call-start = ((), (), s32[]{:S(2)}) async-start(), calls=%async_computation.19 | async-start | bytes 1769472 | tf_op jit(solution)/shard_map/all_gather | solution.py:128
  42.3 185.9 %reduce-scatter.16.cloned.1.call-start = ((), (), s32[]{:S(2)}) async-start(), calls=%async_computation.9 | async-start | bytes 983040 | tf_op jit(solution)/shard_map/reduce_scatter | solution.py:136
  200.8 5.1 copy-start.5
  200.8 5.1 copy-start.44
  200.8 27.4 %copy-start.1 = (bf16[128,768]{1,0:T(8,128)(2,1)S(1)}, bf16[128,768]{1,0:T(8,128)(2,1)}, u32[]{:S(2)}) copy-start(bf16[128,768]{1,0:T(8,128)(2,1)} %param.16) | copy-start | bytes 589828
  202.3 28.1 %copy-start.16 = (bf16[512,3,64]{0,2,1:T(8,128)(2,1)}, bf16[512,3,64]{0,2,1:T(8,128)(2,1)S(1)}, u32[]{:S(2)}) copy-start(bf16[512,3,64]{0,2,1:T(8,128)(2,1)S(1)} %divide_convert_fusion) | copy-start | bytes 589828
  204.7 53.5 %all-gather.12.cloned.1.call-start = ((), (), s32[]{:S(2)}) async-start(), calls=%async_computation.10 | async-start | bytes 2654208 | tf_op jit(solution)/shard_map/all_gather | solution.py:72
  205.3 78.8 %all-gather.14.cloned.1.call-start = ((), (), s32[]{:S(2)}) async-start(), calls=%async_computation.11 | async-start | bytes 1327104 | tf_op jit(solution)/shard_map/all_gather | solution.py:73
  205.9 104.7 %reduce-scatter.18.cloned.1.call-start = ((), (), s32[]{:S(2)}) async-start(), calls=%async_computation.12 | async-start | bytes 983040 | tf_op jit(solution)/shard_map/reduce_scatter | solution.py:151
  225.7 84.8 %copy-start.26 = (f32[768]{0:T(1024)}, f32[768]{0:T(1024)S(1)}, u32[]{:S(2)}) copy-start(f32[768]{0:T(1024)S(1)} %get-tuple-element.605) | copy-start | bytes 9220
  229.3 81.3 %copy-start.32 = (f32[128]{0:T(128)}, f32[128]{0:T(128)S(1)}, u32[]{:S(2)}) copy-start(f32[128]{0:T(128)S(1)} %broadcast_multiply_fusion.1) | copy-start | bytes 1540
  230.4 30.0 %copy-start.42 = (f32[128]{0:T(128)}, f32[128]{0:T(128)S(1)}, u32[]{:S(2)}) copy-start(f32[128]{0:T(128)S(1)} %multiply_reduce_fusion.4) | copy-start | bytes 1540
  230.4 80.1 %copy-start.35 = (f32[128]{0:T(128)}, f32[128]{0:T(128)S(1)}, u32[]{:S(2)}) copy-start(f32[128]{0:T(128)S(1)} %fusion.91) | copy-start | bytes 1540
  249.6 10.8 %copy-start.21 = (bf16[512,768]{1,0:T(8,128)(2,1)}, bf16[512,768]{1,0:T(8,128)(2,1)S(1)}, u32[]{:S(2)}) copy-start(bf16[512,768]{1,0:T(8,128)(2,1)S(1)} %all_gather.57) | copy-start | bytes 2359300
  266.9 20.1 %copy-start.13 = (bf16[512,768]{1,0:T(8,128)(2,1)}, bf16[512,768]{1,0:T(8,128)(2,1)S(1)}, u32[]{:S(2)}) copy-start(bf16[512,768]{1,0:T(8,128)(2,1)S(1)} %get-tuple-element.698) | copy-start | bytes 2359300
  284.1 26.5 %copy-start.4 = (bf16[128,768]{1,0:T(8,128)(2,1)S(1)}, bf16[128,768]{1,0:T(8,128)(2,1)}, u32[]{:S(2)}) copy-start(bf16[128,768]{1,0:T(8,128)(2,1)} %reduce-scatter.16.cloned.1.call-done) | copy-start | bytes 589828
  287.1 25.0 %copy-start.15 = (bf16[128,768]{1,0:T(8,128)(2,1)S(1)}, bf16[128,768]{1,0:T(8,128)(2,1)}, u32[]{:S(2)}) copy-start(bf16[128,768]{1,0:T(8,128)(2,1)} %param.25) | copy-start | bytes 589828
  287.1 52.2 %all-gather.22.cloned.1.call-start = ((), (), s32[]{:S(2)}) async-start(), calls=%async_computation.20 | async-start | bytes 1769472 | tf_op jit(solution)/shard_map/all_gather | solution.py:238
  287.8 76.0 %reduce-scatter.20.cloned.1.call-start = ((), (), s32[]{:S(2)}) async-start(), calls=%async_computation.13 | async-start | bytes 983040 | tf_op jit(solution)/shard_map/reduce_scatter | solution.py:164
  310.5 21.3 %copy-start.57 = (f32[512,768]{1,0:T(8,128)S(1)}, f32[512,768]{1,0:T(8,128)}, u32[]{:S(2)}) copy-start(f32[512,768]{1,0:T(8,128)} %get-tuple-element.699) | copy-start | bytes 4718596
  312.1 19.8 %copy-start.47 = (bf16[768,768]{0,1:T(8,128)(2,1)S(1)}, bf16[768,768]{0,1:T(8,128)(2,1)}, u32[]{:S(2)}) copy-start(bf16[768,768]{0,1:T(8,128)(2,1)} %all-gather.14.cloned.1.call-done) | copy-start | bytes 3538948
  312.1 19.8 %copy-start.52 = (f32[512,768]{1,0:T(8,128)S(1)}, f32[512,768]{1,0:T(8,128)}, u32[]{:S(2)}) copy-start(f32[512,768]{1,0:T(8,128)} %copy-done.51) | copy-start | bytes 4718596
  313.8 21.2 %copy-start.38 = (f32[128]{0:T(128)}, f32[128]{0:T(128)S(1)}, u32[]{:S(2)}) copy-start(f32[128]{0:T(128)S(1)} %negate_multiply_fusion.2) | copy-start | bytes 1540
  337.9 177.6 %all-gather.16.cloned.1.call-start = ((), (), s32[]{:S(2)}) async-start(), calls=%async_computation.14 | async-start | bytes 1769472 | tf_op jit(solution)/shard_map/all_gather | solution.py:239
  341.3 11.9 %copy-start.37 = (bf16[768]{0:T(1024)(128)(2,1)S(1)}, bf16[768]{0:T(1024)(128)(2,1)}, u32[]{:S(2)}) copy-start(bf16[768]{0:T(1024)(128)(2,1)} %get-tuple-element.600) | copy-start | bytes 4612
  341.3 22.5 %copy-start.27 = (f32[768]{0:T(1024)S(1)}, f32[768]{0:T(1024)}, u32[]{:S(2)}) copy-start(f32[768]{0:T(1024)} %copy-done.26) | copy-start | bytes 9220
  341.3 22.5 %copy-start.33 = (f32[128]{0:T(128)S(1)}, f32[128]{0:T(128)}, u32[]{:S(2)}) copy-start(f32[128]{0:T(128)} %copy-done.32) | copy-start | bytes 1540
  341.3 22.5 %copy-start.36 = (f32[128]{0:T(128)S(1)}, f32[128]{0:T(128)}, u32[]{:S(2)}) copy-start(f32[128]{0:T(128)} %copy-done.35) | copy-start | bytes 1540
  341.4 22.4 %copy-start.39 = (f32[128]{0:T(128)S(1)}, f32[128]{0:T(128)}, u32[]{:S(2)}) copy-start(f32[128]{0:T(128)} %copy-done.38) | copy-start | bytes 1540
  341.4 24.3 %copy-start.43 = (f32[128]{0:T(128)S(1)}, f32[128]{0:T(128)}, u32[]{:S(2)}) copy-start(f32[128]{0:T(128)} %copy-done.42) | copy-start | bytes 1540
  343.1 22.6 %copy-start.31 = (f32[3,512]{1,0:T(4,128)}, f32[3,512]{1,0:T(4,128)S(1)}, u32[]{:S(2)}) copy-start(f32[3,512]{1,0:T(4,128)S(1)} %log_add_fusion) | copy-start | bytes 18436
  365.6 20.5 %copy-start.8 = (bf16[192,768]{0,1:T(8,128)(2,1)S(1)}, bf16[192,768]{0,1:T(8,128)(2,1)}, u32[]{:S(2)}) copy-start(bf16[192,768]{0,1:T(8,128)(2,1)} %all_gather.54) | copy-start | bytes 884740
  366.9 20.3 %copy-start.6 = (f32[128,768]{1,0:T(8,128)}, f32[128,768]{1,0:T(8,128)S(1)}, u32[]{:S(2)}) copy-start(f32[128,768]{1,0:T(8,128)S(1)} %get-tuple-element.693) | copy-start | bytes 1179652
  366.9 19.6 %copy-start.18 = (f32[512,3,64]{0,2,1:T(8,128)S(1)}, f32[512,3,64]{0,2,1:T(8,128)}, u32[]{:S(2)}) copy-start(f32[512,3,64]{0,2,1:T(8,128)} %get-tuple-element.226) | copy-start | bytes 1179652
  366.9 19.6 %copy-start.25 = (f32[3,512]{1,0:T(4,128)S(1)}, f32[3,512]{1,0:T(4,128)}, u32[]{:S(2)}) copy-start(f32[3,512]{1,0:T(4,128)} %copy-done.23) | copy-start | bytes 18436
  367.0 20.3 %copy-start.40 = (f32[128]{0:T(128)}, f32[128]{0:T(128)S(1)}, u32[]{:S(2)}) copy-start(f32[128]{0:T(128)S(1)} %negate_multiply_fusion.1) | copy-start | bytes 1540
  387.3 283.0 %reduce-scatter.32.cloned.1.call-start = ((), (), s32[]{:S(2)}) async-start(), calls=%async_computation.23 | async-start | bytes 442368
  488.0 14.9 %copy-start.3 = (bf16[512,768]{1,0:T(8,128)(2,1)S(1)}, bf16[512,768]{1,0:T(8,128)(2,1)}, u32[]{:S(2)}) copy-start(bf16[512,768]{1,0:T(8,128)(2,1)} %copy-done.2) | copy-start | bytes 2359300
  505.2 166.6 %reduce-scatter.30.cloned.1.call-start = ((), (), s32[]{:S(2)}) async-start(), calls=%async_computation.22 | async-start | bytes 884736
  515.4 164.1 %reduce-scatter.22.cloned.1.call-start = ((), (), s32[]{:S(2)}) async-start(), calls=%async_computation.15 | async-start | bytes 983040 | tf_op jit(solution)/shard_map/reduce_scatter | solution.py:249
  658.8 66.4 %reduce-scatter.26.cloned.1.call-start = ((), (), s32[]{:S(2)}) async-start(), calls=%async_computation.17 | async-start | bytes 2654208 | tf_op jit(solution)/shard_map/reduce_scatter | solution.py:261
  661.2 108.6 %reduce-scatter.28.cloned.1.call-start = ((), (), s32[]{:S(2)}) async-start(), calls=%async_computation.21 | async-start | bytes 2211840
  664.9 162.7 %reduce-scatter.24.cloned.1.call-start = ((), (), s32[]{:S(2)}) async-start(), calls=%async_computation.16 | async-start | bytes 5308416 | tf_op jit(solution)/shard_map/reduce_scatter | solution.py:260
  670.3 9.2 %copy-start.7 = (f32[128,768]{1,0:T(8,128)S(1)}, f32[128,768]{1,0:T(8,128)}, u32[]{:S(2)}) copy-start(f32[128,768]{1,0:T(8,128)} %copy-done.6) | copy-start | bytes 1179652
  670.3 9.2 %copy-start.41 = (f32[128]{0:T(128)S(1)}, f32[128]{0:T(128)}, u32[]{:S(2)}) copy-start(f32[128]{0:T(128)} %copy-done.40) | copy-start | bytes 1540
  (39 other events, 94.9 us)
Sparse Core Ops, SparseCore 0:
  41.6 24.7 all-gather.17
  68.9 25.8 all-gather.19
  204.8 23.3 reduce-scatter.15
  229.9 28.2 all-gather.11
  260.0 24.0 all-gather.13
  287.2 23.2 reduce-scatter.17
  313.0 25.1 all-gather.21
  340.5 23.2 reduce-scatter.19
  387.4 25.1 all-gather.15
  505.3 31.9 reduce-scatter.31
  540.5 34.9 reduce-scatter.29
  658.9 20.5 reduce-scatter.21
  683.4 41.7 reduce-scatter.25
  729.4 40.2 reduce-scatter.27
  773.6 53.8 reduce-scatter.23

commit v2 on v1

--- a/solution.py
+++ b/solution.py
@@ -1,6 +1,8 @@
 import jax
 import jax.numpy as jnp
 from jax import lax
+from jax.experimental import pallas as pl
+from jax.experimental.pallas import tpu as pltpu
 from jax.sharding import PartitionSpec as P
 
 HEADS = 12
@@ -264,6 +266,321 @@
     return (result.astype(jnp.bfloat16), input_grad, s_qkv, s_out, s_gu, s_down, s_norm)
 
 
+Q_SLOTS = 32
+K_SLOTS = 16
+SEQ_STEP = 65536.0
+FAR = 32768.0
+LANE_OF = (0, 64, 192)
+
+
+def by_head(rows, lanes):
+    lane = lax.broadcasted_iota(jnp.int32, rows.shape, 1)
+    parts = [jnp.where((lane >= first) & (lane < first + HEAD_DIM), rows, 0.0) for first in lanes]
+    return jnp.concatenate(parts, axis=0).astype(jnp.bfloat16)
+
+
+def key_tiles(kv_ref, j):
+    rows = kv_ref.shape[0] * K_SLOTS
+    blk = kv_ref[:, pl.ds(pl.multiple_of(j * K_SLOTS, K_SLOTS), K_SLOTS), :]
+    return blk.reshape(rows, blk.shape[2])
+
+
+def attend(span_ref, slope_ref, q_ref, kv_ref, kcode_ref, qcode_ref, out_ref, lse_ref, vt_ref):
+    devs, slots, _ = kv_ref.shape
+    rows = devs * K_SLOTS
+    q_rows = q_ref.shape[0] * Q_SLOTS
+
+    def turn(j, _):
+        kv = key_tiles(kv_ref, j)[:, 128:384]
+        vt_ref[j] = kv.astype(jnp.float32).T.astype(jnp.bfloat16)
+        return 0
+
+    lax.fori_loop(0, slots // K_SLOTS, turn, 0)
+
+    def chunk(i, _):
+        first = pl.multiple_of(i * Q_SLOTS, Q_SLOTS)
+        q = q_ref[:, pl.ds(first, Q_SLOTS), :].reshape(q_rows, 192).astype(jnp.float32)
+        q = jnp.concatenate([q, jnp.zeros((q_rows, 64), jnp.float32)], axis=1)
+        qbd = by_head(q, (0, 64, 128))
+        qcode = qcode_ref[i]
+
+        def block(j, state):
+            kv = key_tiles(kv_ref, j)
+            keys = jnp.concatenate([kv[:, 0:128], kv[:, 256:384]], axis=1)
+            s_all = lax.dot_general(keys, qbd, (((1,), (1,)), ((), ())), preferred_element_type=jnp.float32)
+            dist = jnp.abs(kcode_ref[pl.ds(pl.multiple_of(j * rows, rows), rows), :] - qcode)
+            keep = dist < FAR
+            fresh = []
+            for h in range(3):
+                best, total, acc = state[h]
+                s = jnp.where(keep, s_all[:, 128 * h : 128 * h + 128] - slope_ref[h] * dist, masked_score)
+                top = jnp.maximum(best, jnp.max(s, axis=0, keepdims=True))
+                factor = jnp.exp(best - top)
+                p = jnp.exp(s - top)
+                total = total * factor + jnp.sum(p, axis=0, keepdims=True)
+                vt = vt_ref[j, LANE_OF[h] : LANE_OF[h] + 64, :]
+                acc = acc * factor + jnp.dot(vt, p.astype(jnp.bfloat16), preferred_element_type=jnp.float32)
+                fresh.append((top, total, acc))
+            return tuple(fresh)
+
+        start = tuple(
+            (
+                jnp.full((1, q_rows), masked_score, jnp.float32),
+                jnp.zeros((1, q_rows), jnp.float32),
+                jnp.zeros((64, q_rows), jnp.float32),
+            )
+            for _ in range(3)
+        )
+        done = lax.fori_loop(span_ref[i, 0], span_ref[i, 1], block, start)
+        outs = [acc / total for _, total, acc in done]
+        full = jnp.concatenate([outs[0], outs[1], jnp.zeros((64, q_rows), jnp.float32), outs[2]], axis=0)
+        out_ref[:, pl.ds(first, Q_SLOTS), :] = full.T.astype(jnp.bfloat16).reshape(-1, Q_SLOTS, 256)
+        for h in range(3):
+            lse_ref[i, h : h + 1, :] = done[h][0] + jnp.log(done[h][1])
+        return 0
+
+    lax.fori_loop(0, slots // Q_SLOTS, chunk, 0)
+
+
+def attend_back(span_ref, slope_ref, q_ref, kv_ref, kcode_ref, qcode_ref, out_ref, do_ref, lse_ref,
+                dq_ref, dkv_ref, kt_ref, sum_ref):
+    devs, slots, _ = kv_ref.shape
+    rows = devs * K_SLOTS
+    q_rows = q_ref.shape[0] * Q_SLOTS
+    scale = HEAD_DIM ** (-0.5)
+
+    def turn(j, _):
+        kv = key_tiles(kv_ref, j)
+        keys = jnp.concatenate([kv[:, 0:128], kv[:, 256:384]], axis=1)
+        kt_ref[j] = keys.astype(jnp.float32).T.astype(jnp.bfloat16)
+        sum_ref[j] = jnp.zeros((rows, 384), jnp.float32)
+        return 0
+
+    lax.fori_loop(0, slots // K_SLOTS, turn, 0)
+
+    def chunk(i, _):
+        first = pl.multiple_of(i * Q_SLOTS, Q_SLOTS)
+        q = q_ref[:, pl.ds(first, Q_SLOTS), :].reshape(q_rows, 192).astype(jnp.float32)
+        q = jnp.concatenate([q, jnp.zeros((q_rows, 64), jnp.float32)], axis=1)
+        qbd = by_head(q, (0, 64, 128))
+        do = do_ref[:, pl.ds(first, Q_SLOTS), :].reshape(q_rows, 256).astype(jnp.float32)
+        out = out_ref[:, pl.ds(first, Q_SLOTS), :].reshape(q_rows, 256).astype(jnp.float32)
+        dobd = by_head(do, LANE_OF)
+        prod = (do * out).T
+        delta = [jnp.sum(prod[f : f + 64, :], axis=0, keepdims=True) for f in LANE_OF]
+        qcode = qcode_ref[i]
+
+        def block(j, state):
+            kv = key_tiles(kv_ref, j)
+            keys = jnp.concatenate([kv[:, 0:128], kv[:, 256:384]], axis=1)
+            vals = kv[:, 128:384]
+            s_all = lax.dot_general(keys, qbd, (((1,), (1,)), ((), ())), preferred_element_type=jnp.float32)
+            dp_all = lax.dot_general(vals, dobd, (((1,), (1,)), ((), ())), preferred_element_type=jnp.float32)
+            dist = jnp.abs(kcode_ref[pl.ds(pl.multiple_of(j * rows, rows), rows), :] - qcode)
+            keep = dist < FAR
+            ps, dss, fresh = [], [], []
+            for h in range(3):
+                s = s_all[:, 128 * h : 128 * h + 128] - slope_ref[h] * dist - lse_ref[i, h : h + 1, :]
+                p = jnp.exp(jnp.where(keep, s, masked_score))
+                ds = (p * (dp_all[:, 128 * h : 128 * h + 128] - delta[h])).astype(jnp.bfloat16)
+                ps.append(p.astype(jnp.bfloat16))
+                dss.append(ds)
+                kt = kt_ref[j, 64 * h : 64 * h + 64, :]
+                fresh.append(state[h] + jnp.dot(kt, ds, preferred_element_type=jnp.float32))
+            dv = jnp.dot(jnp.concatenate(ps, axis=1), dobd, preferred_element_type=jnp.float32)
+            dk = jnp.dot(jnp.concatenate(dss, axis=1), qbd, preferred_element_type=jnp.float32)
+            sum_ref[j, :, 0:128] += dk[:, 0:128]
+            sum_ref[j, :, 128:256] += dv[:, 0:128]
+            sum_ref[j, :, 256:384] += dk[:, 128:256] + dv[:, 128:256]
+            return tuple(fresh)
+
+        start = tuple(jnp.zeros((64, q_rows), jnp.float32) for _ in range(3))
+        done = lax.fori_loop(span_ref[i, 0], span_ref[i, 1], block, start)
+        full = jnp.concatenate(done + (jnp.zeros((64, q_rows), jnp.float32),), axis=0) * scale
+        dq_ref[:, pl.ds(first, Q_SLOTS), :] = full.T[:, 0:192].astype(jnp.bfloat16).reshape(-1, Q_SLOTS, 192)
+        return 0
+
+    lax.fori_loop(0, slots // Q_SLOTS, chunk, 0)
+
+    def leave(j, _):
+        dkv_ref[:, pl.ds(pl.multiple_of(j * K_SLOTS, K_SLOTS), K_SLOTS), :] = (
+            sum_ref[j].astype(jnp.bfloat16).reshape(devs, K_SLOTS, 384)
+        )
+        return 0
+
+    lax.fori_loop(0, slots // K_SLOTS, leave, 0)
+
+
+VM = pl.BlockSpec(memory_space=pltpu.VMEM)
+SM = pl.BlockSpec(memory_space=pltpu.SMEM)
+
+
+def run_attend(span, slopes, q, kv, kcode, qcode):
+    heads_n, slots, _ = q.shape
+    devs = kv.shape[0]
+    return pl.pallas_call(
+        attend,
+        out_shape=(
+            jax.ShapeDtypeStruct((heads_n, slots, 256), jnp.bfloat16),
+            jax.ShapeDtypeStruct((slots // Q_SLOTS, 8, heads_n * Q_SLOTS), jnp.float32),
+        ),
+        in_specs=[SM, SM, VM, VM, VM, VM],
+        out_specs=(VM, VM),
+        scratch_shapes=[pltpu.VMEM((slots // K_SLOTS, 256, devs * K_SLOTS), jnp.bfloat16)],
+        compiler_params=pltpu.CompilerParams(vmem_limit_bytes=40 << 20),
+        name="attend",
+    )(span, slopes, q, kv, kcode, qcode)
+
+
+def run_attend_back(span, slopes, q, kv, kcode, qcode, out, do, lse):
+    heads_n, slots, _ = q.shape
+    devs = kv.shape[0]
+    return pl.pallas_call(
+        attend_back,
+        out_shape=(
+            jax.ShapeDtypeStruct((heads_n, slots, 192), jnp.bfloat16),
+            jax.ShapeDtypeStruct((devs, slots, 384), jnp.bfloat16),
+        ),
+        in_specs=[SM, SM, VM, VM, VM, VM, VM, VM, VM],
+        out_specs=(VM, VM),
+        scratch_shapes=[
+            pltpu.VMEM((slots // K_SLOTS, 256, devs * K_SLOTS), jnp.bfloat16),
+            pltpu.VMEM((slots // K_SLOTS, devs * K_SLOTS, 384), jnp.float32),
+        ],
+        compiler_params=pltpu.CompilerParams(vmem_limit_bytes=48 << 20),
+        name="attend_back",
+    )(span, slopes, q, kv, kcode, qcode, out, do, lse)
+
+
+def key_spans(seq_starts, seq_ends, chunk_positions, block_positions, chunks):
+    first = chunk_positions * jnp.arange(chunks, dtype=jnp.int32)
+    last = first + chunk_positions - 1
+    lo_seq = jnp.sum((first[:, None] >= seq_ends[None, :]).astype(jnp.int32), axis=1)
+    hi_seq = jnp.sum((last[:, None] >= seq_ends[None, :]).astype(jnp.int32), axis=1)
+    seqs = jnp.arange(seq_ends.shape[0], dtype=jnp.int32)[None, :]
+    lo = jnp.sum(jnp.where(seqs == lo_seq[:, None], seq_starts[None, :], 0), axis=1)
+    hi = jnp.sum(jnp.where(seqs == hi_seq[:, None], seq_ends[None, :], 0), axis=1)
+    return jnp.stack([lo // block_positions, (hi + block_positions - 1) // block_positions], axis=1)
+
+
+def to_cols(w):
+    p = [[w[:, (h * 3 + c) * 64 : (h * 3 + c) * 64 + 64] for c in range(3)] for h in range(3)]
+    return jnp.concatenate(
+        [p[0][1], p[1][1], p[0][2], p[1][2], p[2][1], p[2][2], p[0][0], p[1][0], p[2][0]], axis=1
+    )
+
+
+def from_cols(g):
+    piece = [g[:, 64 * i : 64 * i + 64] for i in range(9)]
+    order = (6, 0, 2, 7, 1, 3, 8, 4, 5)
+    return jnp.concatenate([piece[i] for i in order], axis=1)
+
+
+def pad_heads(rows):
+    return jnp.concatenate([rows[:128], jnp.zeros((64, rows.shape[1]), rows.dtype), rows[128:]], axis=0)
+
+
+def fast_shards(
+    tokens, w_qkv, w_out, w_gate_up, w_down, norm_params, alibi_slope, lengths, placement, out_grad
+):
+    heads_n = lax.axis_size("head")
+    blk_n = lax.axis_size("blk")
+    head_idx = lax.axis_index("head")
+    blk_idx = lax.axis_index("blk")
+    tok_rows, width = tokens.shape
+    per_dev = HEADS // heads_n
+    group_rows = heads_n * tok_rows
+    devs = heads_n * blk_n
+    share = w_qkv.shape[0]
+    bf16 = jnp.bfloat16
+
+    attn_w = lax.all_gather(jnp.concatenate([to_cols(w_qkv), w_out.T], axis=1), "blk", axis=0, tiled=True)
+    ffn_w = lax.all_gather(
+        jnp.concatenate([w_gate_up, w_down.T[None]], axis=0), "blk", axis=1, tiled=True
+    )
+    norms = lax.all_gather(norm_params.reshape(share), ("blk", "head"), axis=0, tiled=False)
+    norms = norms.reshape(blk_n, heads_n, share).transpose(1, 0, 2).reshape(heads_n, width).astype(jnp.float32)
+    group_tokens = lax.all_gather(tokens, "head", axis=0, tiled=True)
+    w_in = attn_w[:, :576]
+    out_t = attn_w[:, 576:]
+    w_gate, w_up, down_t = ffn_w[0], ffn_w[1], ffn_w[2]
+
+    kvq = jnp.dot(group_tokens, w_in, preferred_element_type=jnp.float32).astype(bf16)
+    kv = lax.all_gather(kvq[:, :384], "blk", axis=0, tiled=True).reshape(devs, tok_rows, 384)
+    q = (kvq[:, 384:] * bf16(HEAD_DIM ** (-0.5))).reshape(heads_n, tok_rows, 192)
+
+    seq_ends = prefix_sums(lengths)
+    code = placement.astype(jnp.float32) + SEQ_STEP * seq_of(placement, seq_ends).astype(jnp.float32)
+    k_blocks = tok_rows // K_SLOTS
+    q_chunks = tok_rows // Q_SLOTS
+    kcode = code.reshape(devs, k_blocks, K_SLOTS).transpose(1, 0, 2).reshape(-1, 1)
+    kcode = jnp.broadcast_to(kcode, (kcode.shape[0], 128))
+    qcode = lax.dynamic_slice_in_dim(code, blk_idx * group_rows, group_rows)
+    qcode = qcode.reshape(heads_n, q_chunks, Q_SLOTS).transpose(1, 0, 2).reshape(q_chunks, 1, heads_n * Q_SLOTS)
+    slopes = lax.dynamic_slice_in_dim(alibi_slope, head_idx * per_dev, per_dev)
+    span = key_spans(seq_ends - lengths, seq_ends, Q_SLOTS * devs, K_SLOTS * devs, q_chunks)
+
+    mixed, lse = run_attend(span, slopes, q, kv, kcode, qcode)
+    mixed_rows = mixed.reshape(group_rows, 256)
+    out_pad = pad_heads(out_t.T)
+    attn_out = lax.psum_scatter(
+        jnp.dot(mixed_rows, out_pad, preferred_element_type=jnp.float32).astype(bf16),
+        "head", scatter_dimension=0, tiled=True,
+    ).astype(jnp.float32)
+    resid_one = tokens.astype(jnp.float32) + attn_out
+    hidden, norm_one_back = jax.vjp(layer_norm, resid_one, norms[0], norms[1])
+    ffn_rows = lax.all_gather(hidden.astype(bf16), "head", axis=0, tiled=True)
+    gate = jnp.dot(ffn_rows, w_gate, preferred_element_type=jnp.float32)
+    upward = jnp.dot(ffn_rows, w_up, preferred_element_type=jnp.float32)
+    gated, geglu_back = jax.vjp(geglu, gate, upward)
+    gated_low = gated.astype(bf16)
+    branch = lax.psum_scatter(
+        dot_back(gated_low, down_t).astype(bf16), "head", scatter_dimension=0, tiled=True
+    ).astype(jnp.float32)
+    result, norm_two_back = jax.vjp(layer_norm, hidden + branch, norms[2], norms[3])
+    d_two, d_gain_two, d_shift_two = norm_two_back(out_grad.astype(jnp.float32))
+    branch_rows = lax.all_gather(d_two.astype(bf16), "head", axis=0, tiled=True)
+    d_gate, d_up = geglu_back(jnp.dot(branch_rows, down_t, preferred_element_type=jnp.float32))
+    d_gate_low = d_gate.astype(bf16)
+    d_up_low = d_up.astype(bf16)
+    hidden_part = dot_back(d_gate_low, w_gate) + dot_back(d_up_low, w_up)
+    d_hidden = d_two + lax.psum_scatter(
+        hidden_part.astype(bf16), "head", scatter_dimension=0, tiled=True
+    ).astype(jnp.float32)
+    g_ffn = jnp.stack(
+        [weight_grad(ffn_rows, d_gate_low), weight_grad(ffn_rows, d_up_low), weight_grad(branch_rows, gated_low)]
+    ).astype(bf16)
+    s_ffn = lax.psum_scatter(g_ffn, "blk", scatter_dimension=1, tiled=True).astype(jnp.float32)
+    d_one, d_gain_one, d_shift_one = norm_one_back(d_hidden)
+    attn_rows = lax.all_gather(d_one.astype(bf16), "head", axis=0, tiled=True)
+    d_heads = dot_back(attn_rows, out_pad).astype(bf16)
+    d_q, dkv = run_attend_back(
+        span, slopes, q, kv, kcode, qcode, mixed, d_heads.reshape(heads_n, tok_rows, 256), lse
+    )
+    d_kv = lax.psum_scatter(dkv.reshape(devs * tok_rows, 384), "blk", scatter_dimension=0, tiled=True)
+    d_kvq = jnp.concatenate([d_kv, d_q.reshape(group_rows, 192)], axis=1)
+    input_grad = d_one + lax.psum_scatter(
+        dot_back(d_kvq, w_in).astype(bf16), "head", scatter_dimension=0, tiled=True
+    ).astype(jnp.float32)
+    g_out_t = weight_grad(attn_rows, mixed_rows)
+    g_attn = jnp.concatenate(
+        [weight_grad(group_tokens, d_kvq), g_out_t[:, :128], g_out_t[:, 192:]], axis=1
+    ).astype(bf16)
+    s_attn = lax.psum_scatter(g_attn, "blk", scatter_dimension=0, tiled=True).astype(jnp.float32)
+    g_norm = jnp.stack([d_gain_one, d_shift_one, d_gain_two, d_shift_two], axis=0)
+    g_norm = g_norm.reshape(heads_n, blk_n, share).transpose(1, 0, 2).reshape(devs, share)
+    s_norm = lax.psum_scatter(g_norm, ("blk", "head"), scatter_dimension=0, tiled=True)
+    return (
+        result.astype(bf16),
+        input_grad,
+        from_cols(s_attn[:, :576]),
+        s_attn[:, 576:].T,
+        s_ffn[:2],
+        s_ffn[2].T,
+        s_norm.reshape(share, 1),
+    )
+
+
 def solution(mesh):
     placed = (
         P(("blk", "head"), None),
@@ -277,8 +594,9 @@
         P(),
         P(("blk", "head"), None),
     )
+    small = mesh.shape["blk"] == 8 and mesh.shape["head"] == 4
     return jax.shard_map(
-        shards,
+        fast_shards if small else shards,
         mesh=mesh,
         in_specs=placed,
         out_specs=(

time: 839 us -> 462 us (0.55)
  matrix products: 199 us -> 27.6 us
  other arithmetic: 86.1 us -> 15.1 us
  waiting for transfers between devices: 252 us -> 184 us
  local copies, waits for them, and re-layouts: 86.4 us -> 22.2 us
  loops' own time: 47.4 us -> 0 us
  Pallas kernels: 0 us -> 41 us
    dot_general x61 -> x5, matrix products: 184 us -> 14.9 us  [the longest x1 5.33 us: fast_shards(): upward = jnp.dot(ffn_rows, w_up, preferred_element_type=jnp.float32)]
    unnamed x1 -> x2, blocking collectives: 10.2 us -> 79.9 us
    all_gather x10 -> x4, blocking collectives: 138 us -> 75.8 us  [the longest x1 21.5 us: fast_shards(): group_tokens = lax.all_gather(tokens, 'head', axis=0, tiled=True)]
    dynamic_slice x58 -> x2, local copies, waits for them, and re-layouts: 58.3 us -> 0.15 us  [the longest x1 0.08 us: fast_shards(): qcode = lax.dynamic_slice_in_dim(code, blk_idx * group_rows, group_rows)]
    another operation x3 -> x0, loops' own time: 47.4 us -> none  [the longest x1 16 us: shards(): lax.scan(forward_per_block, running, split_rows((lax.all_gather(key_rows,...]
    pallas_call x0 -> x2, Pallas kernels: none -> 41 us  [the longest x1 25.9 us: run_attend_back(): pl.pallas_call(attend_back, out_shape=(jax.ShapeDtypeStruct((heads_n, slo...]
    reduce_scatter x6, waiting for transfers between devices: 143 us -> 113 us  [the longest x1 39.3 us: fast_shards(): lax.psum_scatter(dkv.reshape(devs * tok_rows, 384), 'blk', scatter_dimens...]
    all_gather x6 -> x3, waiting for transfers between devices: 61.9 us -> 34 us  [the longest x1 28.6 us: fast_shards(): lax.all_gather(kvq[:, :384], 'blk', axis=0, tiled=True)]
  transfers between devices with their start and end apart: 15 -> 10, of which waited for: 11 -> 8; matrix products, arithmetic and copies ran while one was open for 32% -> 6% of each run, Pallas kernels for 0% -> 0%
where the time goes in v2:
time: 462 us; the launch traced here: 461 us
  waiting for transfers between devices  184 us (40%)
  blocking collectives  156 us (34%)
  Pallas kernels  41 us (9%)
  matrix products  27.6 us (6%)
  local copies, waits for them, and re-layouts  22.2 us (5%)
  other arithmetic  15.1 us (3%)
  between operations  14.8 us (3%)
    unnamed x2, blocking collectives  79.9 us
    reduce_scatter x1, waiting for transfers between devices, fast_shards(): lax.psum_scatter(dkv.reshape(devs * tok_rows, 384), 'blk', scatter_dimens...  39.3 us
    unnamed x11, waiting for transfers between devices  37.9 us
    all_gather x1, waiting for transfers between devices, fast_shards(): lax.all_gather(kvq[:, :384], 'blk', axis=0, tiled=True)  28.6 us
    pallas_call x1, Pallas kernels, run_attend_back(): pl.pallas_call(attend_back, out_shape=(jax.ShapeDtypeStruct((heads_n, slo...  25.9 us
    reduce_scatter x1, waiting for transfers between devices, fast_shards(): lax.psum_scatter(dot_back(gated_low, down_t).astype(bf16), 'head', scatte...  23.1 us
    reduce_scatter x1, waiting for transfers between devices, fast_shards(): lax.psum_scatter(hidden_part.astype(bf16), 'head', scatter_dimension=0, t...  22.7 us
    reduce_scatter x1, waiting for transfers between devices, fast_shards(): lax.psum_scatter(dot_back(d_kvq, w_in).astype(bf16), 'head', scatter_dime...  22.3 us
  transfers between devices with their start and end apart: 10, of which 8 were waited for; matrix products, arithmetic and copies ran while one was open for 6% of the time, Pallas kernels for 0%

profile of v2, /device:TPU:0, one launch (start us, length us, event | category | flops | bytes accessed | tf_op | source)
XLA Modules:
  0.0 461.3 jit_solution(2411703058218346946)
XLA Ops:
  7.2 0.9 fusion.41
  8.2 0.9 slice.126
  9.0 0.9 copy.79
  10.8 21.5 %all_gather.25 = bf16[512,768]{1,0:T(8,128)(2,1)S(1)} all-gather(bf16[128,768]{1,0:T(8,128)(2,1)} %param.10), channel_id=1, replica_groups=mesh['blk'=8,'head'=4] {'head'}, dimensions={0}, use_global_device_ids=true | all-gather | bytes 983040 | tf_op jit(solution)/shard_map/all_gather | solution.py:503
  32.3 5.3 %all-gather.5.cloned.1.call-done = bf16[768,768]{1,0:T(8,128)(2,1)} async-done(((bf16[96,768]{1,0:T(8,128)(2,1)}), bf16[768,768]{1,0:T(8,128)(2,1)}) %all-gather.5.cloned.1.call-update) | async-done | bytes 1179664 | tf_op jit(solution)/shard_map/all_gather | solution.py:497
  37.7 2.0 fusion.10
  42.1 1.2 slice_bitcast_fusion.9
  44.8 28.6 %all-gather.7.cloned.1.call-done = bf16[4096,384]{0,1:T(8,128)(2,1)} async-done(((bf16[512,384]{0,1:T(8,128)(2,1)}), bf16[4096,384]{0,1:T(8,128)(2,1)}) %all-gather.7.cloned.1.call-update) | async-done | bytes 3145744 | tf_op jit(solution)/shard_map/all_gather | solution.py:509
  73.5 3.5 copy.81
  77.6 15.1 %attend.1 = (bf16[4,128,256]{2,1,0:T(8,128)(2,1)S(1)}, f32[4,8,128]{2,1,0:T(8,128)S(1)}) custom-call(s32[4,2]{1,0:T(4,128)S(1)} %pad_add_fusion.span_ref, f32[3]{0:T(128)S(1)} %dynamic_slice.6.slope_ref, bf16[4,128,192]{2,1,0:T(8,128)(2,1)S(1)} %bitcast.77, bf16[32,128,384]{2,1,0:T(8,128)(2,1)S(1)} %bitcast.75, f32[4096,128]{1,0:T(8,128)S(1)} %broadcast_in_dim.76.kcode_ref, ...), custom_call_target="tpu_custom_call" | custom-call | tf_op jit(solution)/shard_map/attend/pallas_call | solution.py:421
  92.8 1.4 convolution_convert_fusion.6
  95.1 0.8 pad_maximum_fusion.3
  96.2 40.5 %all-reduce = bf16[3072]{0:T(1024)(128)(2,1)S(1)} all-reduce(bf16[3072]{0:T(1024)(128)(2,1)S(1)} %dynamic-update-slice), channel_id=2, replica_groups=mesh['blk'=8,'head'=4] {'blk','head'}, use_global_device_ids=true, to_apply=%add | all-reduce | flops 3072 | bytes 12288
  137.0 1.1 fusion.22
  138.1 1.1 multiply_reduce_fusion.3
  139.2 1.1 fusion.23
  140.3 18.0 %all_gather.28 = bf16[512,768]{1,0:T(8,128)(2,1)S(1)} all-gather(bf16[128,768]{1,0:T(8,128)(2,1)S(1)} %fusion.23), channel_id=1, replica_groups=mesh['blk'=8,'head'=4] {'head'}, dimensions={0}, use_global_device_ids=true | all-gather | bytes 983040 | tf_op jit(solution)/shard_map/all_gather | solution.py:532
  158.3 2.2 fusion.12
  160.6 5.3 %multiply_convert_fusion.1 = (bf16[512,768]{1,0:T(8,128)(2,1)S(1)}, f32[512,768]{1,0:T(8,128)}, f32[512,768]{1,0:T(8,128)}) fusion(f32[512,768]{1,0:T(8,128)S(1)} %fusion.12, bf16[512,768]{1,0:T(8,128)(2,1)S(1)} %all_gather.28, bf16[3,768,768]{2,1,0:T(8,128)(2,1)S(1)} %copy-done.18), kind=kOutput, calls=%fused_computation.6 | convolution fusion | flops 629932032 | bytes 7471104 | tf_op jit(solution)/shard_map/dot_general | solution.py:534
  166.0 1.7 convolution_convert_fusion.4
  167.9 23.1 %reduce-scatter.12.cloned.1.call-done = bf16[128,768]{1,0:T(8,128)(2,1)} async-done(((bf16[512,768]{1,0:T(8,128)(2,1)}), bf16[128,768]{1,0:T(8,128)(2,1)}) %reduce-scatter.12.cloned.1.call-update) | async-done | bytes 196624 | tf_op jit(solution)/shard_map/reduce_scatter | solution.py:537
  191.0 1.2 fusion.39
  192.7 0.9 fusion.38
  193.7 18.2 %all_gather.30 = bf16[512,768]{1,0:T(8,128)(2,1)S(1)} all-gather(bf16[128,768]{1,0:T(8,128)(2,1)S(1)} %add_convert_fusion.4), channel_id=1, replica_groups=mesh['blk'=8,'head'=4] {'head'}, dimensions={0}, use_global_device_ids=true | all-gather | bytes 983040 | tf_op jit(solution)/shard_map/all_gather | solution.py:542
  211.9 4.0 multiply_convert_fusion
  215.9 0.8 fusion.11
  217.0 1.7 add_convert_fusion
  218.8 22.7 %reduce-scatter.14.cloned.1.call-done = bf16[128,768]{1,0:T(8,128)(2,1)} async-done(((bf16[512,768]{1,0:T(8,128)(2,1)}), bf16[128,768]{1,0:T(8,128)(2,1)}) %reduce-scatter.14.cloned.1.call-update) | async-done | bytes 196624 | tf_op jit(solution)/shard_map/reduce_scatter | solution.py:547
  241.5 1.2 multiply_reduce_fusion
  242.8 1.3 fusion.37
  244.2 18.1 %all_gather.31 = bf16[512,768]{1,0:T(8,128)(2,1)S(1)} all-gather(bf16[128,768]{1,0:T(8,128)(2,1)S(1)} %add_convert_fusion.3), channel_id=1, replica_groups=mesh['blk'=8,'head'=4] {'head'}, dimensions={0}, use_global_device_ids=true | all-gather | bytes 983040 | tf_op jit(solution)/shard_map/all_gather | solution.py:555
  262.8 25.9 %attend_back.1 = (bf16[4,128,192]{2,1,0:T(8,128)(2,1)S(1)}, bf16[32,128,384]{2,1,0:T(8,128)(2,1)}) custom-call(s32[4,2]{1,0:T(4,128)S(1)} %pad_add_fusion.span_ref, f32[3]{0:T(128)S(1)} %dynamic_slice.6.slope_ref, bf16[4,128,192]{2,1,0:T(8,128)(2,1)S(1)} %bitcast.78, bf16[32,128,384]{2,1,0:T(8,128)(2,1)} %bitcast.76, f32[4096,128]{1,0:T(8,128)S(1)} %copy-done.2, ...), custom_call_target="tpu_custom_call" | custom-call | tf_op jit(solution)/shard_map/attend_back/pallas_call | solution.py:438
  288.8 2.2 fusion.8
  291.0 0.8 fusion.7
  292.2 0.8 fusion.6
  293.0 2.0 pad_maximum_fusion
  295.0 39.3 %reduce-scatter.16.cloned.1.call-done = bf16[512,384]{1,0:T(8,128)(2,1)} async-done(((bf16[4096,384]{1,0:T(8,128)(2,1)}), bf16[512,384]{1,0:T(8,128)(2,1)}) %reduce-scatter.16.cloned.1.call-update) | async-done | bytes 393232 | tf_op jit(solution)/shard_map/reduce_scatter | solution.py:560
  334.4 3.0 convolution_convert_fusion.5
  339.4 1.5 copy.85
  341.2 39.5 %all-reduce.1 = f32[32,96]{1,0:T(8,128)S(1)} all-reduce(f32[32,96]{1,0:T(8,128)S(1)} %bitcast.89), channel_id=10, replica_groups=mesh['blk'=8,'head'=4] {'blk','head'}, use_global_device_ids=true, to_apply=%region_25.26.clone | all-reduce | flops 3072 | bytes 24576
  381.2 5.2 %reduce-scatter.20.cloned.1.call-done = bf16[3,96,768]{2,1,0:T(8,128)(2,1)} async-done(((bf16[3,768,768]{2,1,0:T(8,128)(2,1)}), bf16[3,96,768]{2,1,0:T(8,128)(2,1)}) %reduce-scatter.20.cloned.1.call-update) | async-done | bytes 442384 | tf_op jit(solution)/shard_map/reduce_scatter | solution.py:553
  386.4 1.8 slice.180
  388.2 1.1 convert_element_type.122
  390.1 22.3 %reduce-scatter.18.cloned.1.call-done = bf16[128,768]{1,0:T(8,128)(2,1)} async-done(((bf16[512,768]{1,0:T(8,128)(2,1)}), bf16[128,768]{1,0:T(8,128)(2,1)}) %reduce-scatter.18.cloned.1.call-update) | async-done | bytes 196624 | tf_op jit(solution)/shard_map/reduce_scatter | solution.py:562
  412.3 1.8 convert_add_fusion
  414.1 37.7 %reduce-scatter.22.cloned.1.call-done = bf16[96,768]{1,0:T(8,128)(2,1)} async-done(((bf16[768,768]{1,0:T(8,128)(2,1)}), bf16[96,768]{1,0:T(8,128)(2,1)}) %reduce-scatter.22.cloned.1.call-update) | async-done | bytes 147472
  451.8 1.1 copy.86
  453.6 0.9 copy.84
  (156 shorter events, 13.4 us)
Async XLA Ops:
  7.2 30.5 %all-gather.5.cloned.1.call-start = ((), (), s32[]{:S(2)}) async-start(), calls=%async_computation.7 | async-start | bytes 1327104 | tf_op jit(solution)/shard_map/all_gather | solution.py:497
  10.8 62.7 %all-gather.7.cloned.1.call-start = ((), (), s32[]{:S(2)}) async-start(), calls=%async_computation.8 | async-start | bytes 3538944 | tf_op jit(solution)/shard_map/all_gather | solution.py:509
  32.3 8.1 %copy-start.8 = (bf16[512,768]{1,0:T(8,128)(2,1)}, bf16[512,768]{1,0:T(8,128)(2,1)S(1)}, u32[]{:S(2)}) copy-start(bf16[512,768]{1,0:T(8,128)(2,1)S(1)} %all_gather.25) | copy-start | bytes 2359300
  32.3 8.2 %copy-start.21 = (s32[8]{0:T(128)S(1)}, s32[8]{0:T(128)}, u32[]{:S(2)}) copy-start(s32[8]{0:T(128)} %param.17) | copy-start | bytes 100
  32.3 9.0 %copy-start.17 = (s32[4096]{0:T(1024)S(1)}, s32[4096]{0:T(1024)}, u32[]{:S(2)}) copy-start(s32[4096]{0:T(1024)} %param.18) | copy-start | bytes 49156
  39.6 2.3 copy-start.22
  40.5 96.5 %reduce-scatter.10.cloned.1.call-start = ((), (), s32[]{:S(2)}) async-start(), calls=%async_computation.9 | async-start | bytes 983040 | tf_op jit(solution)/shard_map/reduce_scatter | solution.py:526
  77.0 15.8 %copy-start = (bf16[4096,384]{1,0:T(8,128)(2,1)}, bf16[4096,384]{1,0:T(8,128)(2,1)S(1)}, u32[]{:S(2)}) copy-start(bf16[4096,384]{1,0:T(8,128)(2,1)S(1)} %copy.81) | copy-start | bytes 9437188
  77.6 15.2 %copy-start.1 = (f32[4096,128]{1,0:T(8,128)}, f32[4096,128]{1,0:T(8,128)S(1)}, u32[]{:S(2)}) copy-start(f32[4096,128]{1,0:T(8,128)S(1)} %broadcast_in_dim.76.kcode_ref) | copy-start | bytes 6291460
  77.6 15.2 %copy-start.12 = (bf16[64,768]{0,1:T(8,128)(2,1)S(1)}, bf16[64,768]{0,1:T(8,128)(2,1)}, u32[]{:S(2)}) copy-start(bf16[64,768]{0,1:T(8,128)(2,1)} %slice.161) | copy-start | bytes 294916
  77.6 15.2 %copy-start.14 = (bf16[128,768]{0,1:T(8,128)(2,1)S(1)}, bf16[128,768]{0,1:T(8,128)(2,1)}, u32[]{:S(2)}) copy-start(bf16[128,768]{0,1:T(8,128)(2,1)} %slice.160) | copy-start | bytes 589828
  92.8 2.3 copy-start.11
  92.8 2.3 copy-start.16
  92.8 3.2 copy-start.23
  92.8 44.2 %copy-start.5 = (bf16[128,768]{1,0:T(8,128)(2,1)S(1)}, bf16[128,768]{1,0:T(8,128)(2,1)}, u32[]{:S(2)}) copy-start(bf16[128,768]{1,0:T(8,128)(2,1)} %param.10) | copy-start | bytes 589828
  94.3 0.7 copy-start.3
  95.0 63.3 %all-gather.9.cloned.1.call-start = ((), (), s32[]{:S(2)}) async-start(), calls=%async_computation.10 | async-start | bytes 3981312 | tf_op jit(solution)/shard_map/all_gather | solution.py:498
  95.9 95.1 %reduce-scatter.12.cloned.1.call-start = ((), (), s32[]{:S(2)}) async-start(), calls=%async_computation.11 | async-start | bytes 983040 | tf_op jit(solution)/shard_map/reduce_scatter | solution.py:537
  158.3 2.4 copy-start.18
  160.6 5.3 %copy-start.24 = (f32[512,768]{1,0:T(8,128)}, f32[512,768]{1,0:T(8,128)S(1)}, u32[]{:S(2)}) copy-start(f32[512,768]{1,0:T(8,128)S(1)} %fusion.12) | copy-start | bytes 4718596
  166.0 1.7 copy-start.29
  166.0 25.1 %copy-start.6 = (bf16[128,768]{1,0:T(8,128)(2,1)S(1)}, bf16[128,768]{1,0:T(8,128)(2,1)}, u32[]{:S(2)}) copy-start(bf16[128,768]{1,0:T(8,128)(2,1)} %reduce-scatter.10.cloned.1.call-done) | copy-start | bytes 589828
  167.7 24.7 %copy-start.7 = (bf16[128,768]{1,0:T(8,128)(2,1)S(1)}, bf16[128,768]{1,0:T(8,128)(2,1)}, u32[]{:S(2)}) copy-start(bf16[128,768]{1,0:T(8,128)(2,1)} %param.19) | copy-start | bytes 589828
  167.7 73.8 %reduce-scatter.14.cloned.1.call-start = ((), (), s32[]{:S(2)}) async-start(), calls=%async_computation.12 | async-start | bytes 983040 | tf_op jit(solution)/shard_map/reduce_scatter | solution.py:547
  192.2 19.7 %copy-start.19 = (bf16[3,768,768]{2,1,0:T(8,128)(2,1)S(1)}, bf16[3,768,768]{2,1,0:T(8,128)(2,1)}, u32[]{:S(2)}) copy-start(bf16[3,768,768]{2,1,0:T(8,128)(2,1)} %all-gather.9.cloned.1.call-done) | copy-start | bytes 10616836
  211.9 4.0 copy-start.10
  215.9 0.9 copy-start.27
  215.9 1.1 copy-start.25
  218.8 115.6 %reduce-scatter.16.cloned.1.call-start = ((), (), s32[]{:S(2)}) async-start(), calls=%async_computation.13 | async-start | bytes 3538944 | tf_op jit(solution)/shard_map/reduce_scatter | solution.py:560
  242.7 19.6 %copy-start.13 = (bf16[64,768]{0,1:T(8,128)(2,1)S(1)}, bf16[64,768]{0,1:T(8,128)(2,1)}, u32[]{:S(2)}) copy-start(bf16[64,768]{0,1:T(8,128)(2,1)} %slice.161) | copy-start | bytes 294916
  242.8 19.6 %copy-start.15 = (bf16[128,768]{0,1:T(8,128)(2,1)S(1)}, bf16[128,768]{0,1:T(8,128)(2,1)}, u32[]{:S(2)}) copy-start(bf16[128,768]{0,1:T(8,128)(2,1)} %slice.160) | copy-start | bytes 589828
  244.2 18.6 %copy-start.2 = (f32[4096,128]{1,0:T(8,128)S(1)}, f32[4096,128]{1,0:T(8,128)}, u32[]{:S(2)}) copy-start(f32[4096,128]{1,0:T(8,128)} %copy-done.1) | copy-start | bytes 6291460
  244.2 18.6 %copy-start.4 = (bf16[4,128,256]{2,1,0:T(8,128)(2,1)S(1)}, bf16[4,128,256]{2,1,0:T(8,128)(2,1)}, u32[]{:S(2)}) copy-start(bf16[4,128,256]{2,1,0:T(8,128)(2,1)} %copy-done.3) | copy-start | bytes 786436
  288.7 97.7 %reduce-scatter.20.cloned.1.call-start = ((), (), s32[]{:S(2)}) async-start(), calls=%async_computation.15 | async-start | bytes 3981312 | tf_op jit(solution)/shard_map/reduce_scatter | solution.py:553
  288.7 2.3 copy-start.26
  291.0 1.1 copy-start.28
  295.0 117.3 %reduce-scatter.18.cloned.1.call-start = ((), (), s32[]{:S(2)}) async-start(), calls=%async_computation.14 | async-start | bytes 983040 | tf_op jit(solution)/shard_map/reduce_scatter | solution.py:562
  337.4 1.1 copy-start.9
  337.4 1.2 copy-start.20
  337.4 114.4 %reduce-scatter.22.cloned.1.call-start = ((), (), s32[]{:S(2)}) async-start(), calls=%async_computation.16 | async-start | bytes 1327104
Sparse Core Ops, SparseCore 0:
  10.9 26.7 all-gather.4
  40.6 32.8 all-gather.6
  95.1 23.5 reduce-scatter.9
  121.0 33.9 all-gather.8
  167.8 23.1 reduce-scatter.11
  218.9 22.5 reduce-scatter.13
  288.8 45.4 reduce-scatter.15
  338.2 48.1 reduce-scatter.19
  388.8 23.4 reduce-scatter.17
  415.7 36.0 reduce-scatter.21

commit v3 on v2

--- a/solution.py
+++ b/solution.py
@@ -299,8 +299,7 @@
 
     def chunk(i, _):
         first = pl.multiple_of(i * Q_SLOTS, Q_SLOTS)
-        q = q_ref[:, pl.ds(first, Q_SLOTS), :].reshape(q_rows, 192).astype(jnp.float32)
-        q = jnp.concatenate([q, jnp.zeros((q_rows, 64), jnp.float32)], axis=1)
+        q = q_ref[:, pl.ds(first, Q_SLOTS), :].reshape(q_rows, 256).astype(jnp.float32)
         qbd = by_head(q, (0, 64, 128))
         qcode = qcode_ref[i]
 
@@ -360,8 +359,7 @@
 
     def chunk(i, _):
         first = pl.multiple_of(i * Q_SLOTS, Q_SLOTS)
-        q = q_ref[:, pl.ds(first, Q_SLOTS), :].reshape(q_rows, 192).astype(jnp.float32)
-        q = jnp.concatenate([q, jnp.zeros((q_rows, 64), jnp.float32)], axis=1)
+        q = q_ref[:, pl.ds(first, Q_SLOTS), :].reshape(q_rows, 256).astype(jnp.float32)
         qbd = by_head(q, (0, 64, 128))
         do = do_ref[:, pl.ds(first, Q_SLOTS), :].reshape(q_rows, 256).astype(jnp.float32)
         out = out_ref[:, pl.ds(first, Q_SLOTS), :].reshape(q_rows, 256).astype(jnp.float32)
@@ -397,7 +395,7 @@
         start = tuple(jnp.zeros((64, q_rows), jnp.float32) for _ in range(3))
         done = lax.fori_loop(span_ref[i, 0], span_ref[i, 1], block, start)
         full = jnp.concatenate(done + (jnp.zeros((64, q_rows), jnp.float32),), axis=0) * scale
-        dq_ref[:, pl.ds(first, Q_SLOTS), :] = full.T[:, 0:192].astype(jnp.bfloat16).reshape(-1, Q_SLOTS, 192)
+        dq_ref[:, pl.ds(first, Q_SLOTS), :] = full.T.astype(jnp.bfloat16).reshape(-1, Q_SLOTS, 256)
         return 0
 
     lax.fori_loop(0, slots // Q_SLOTS, chunk, 0)
@@ -438,7 +436,7 @@
     return pl.pallas_call(
         attend_back,
         out_shape=(
-            jax.ShapeDtypeStruct((heads_n, slots, 192), jnp.bfloat16),
+            jax.ShapeDtypeStruct((heads_n, slots, 256), jnp.bfloat16),
             jax.ShapeDtypeStruct((devs, slots, 384), jnp.bfloat16),
         ),
         in_specs=[SM, SM, VM, VM, VM, VM, VM, VM, VM],
@@ -463,21 +461,180 @@
     return jnp.stack([lo // block_positions, (hi + block_positions - 1) // block_positions], axis=1)
 
 
-def to_cols(w):
-    p = [[w[:, (h * 3 + c) * 64 : (h * 3 + c) * 64 + 64] for c in range(3)] for h in range(3)]
-    return jnp.concatenate(
-        [p[0][1], p[1][1], p[0][2], p[1][2], p[2][1], p[2][2], p[0][0], p[1][0], p[2][0]], axis=1
-    )
-
-
-def from_cols(g):
-    piece = [g[:, 64 * i : 64 * i + 64] for i in range(9)]
-    order = (6, 0, 2, 7, 1, 3, 8, 4, 5)
-    return jnp.concatenate([piece[i] for i in order], axis=1)
-
-
-def pad_heads(rows):
-    return jnp.concatenate([rows[:128], jnp.zeros((64, rows.shape[1]), rows.dtype), rows[128:]], axis=0)
+MESH = pl.DeviceIdType.MESH
+
+
+def dot_tn(left, right):
+    return lax.dot_general(left, right, (((0,), (0,)), ((), ())), preferred_element_type=jnp.float32)
+
+
+def dot_nt(left, right):
+    return lax.dot_general(left, right, (((1,), (1,)), ((), ())), preferred_element_type=jnp.float32)
+
+
+def greet(peers):
+    barrier = pltpu.get_barrier_semaphore()
+    for peer in peers:
+        pl.semaphore_signal(barrier, inc=1, device_id=peer, device_id_type=MESH)
+    pl.semaphore_wait(barrier, len(peers))
+
+
+def remote(src, dst, sems, i, peer):
+    return pltpu.make_async_remote_copy(
+        src_ref=src, dst_ref=dst, send_sem=sems.at[0, i], recv_sem=sems.at[1, i],
+        device_id=peer, device_id_type=MESH,
+    )
+
+
+def finish(
+    dkv_ref, dq_ref, tok_ref, w_ref, datt_ref, mixed_ref, done_ref, gffn_ref, gn_ref,
+    dx_ref, sattn_ref, sffn_ref, snorm_ref,
+    kv_sib, kv_sum, kv_in, ffn_sib, ffn_sum, ffn_in, gat, gat_sib, gat_sum, gat_in,
+    part, part_in, att, dkvq, nz_in, nrow, np_in, sems,
+):
+    b = lax.axis_index("blk")
+    z = lax.axis_index("head")
+    chip, core = b // 2, b % 2
+    sib = (chip * 2 + 1 - core, z)
+    flat = [((chip ^ r) * 2 + core, z) for r in (1, 2, 3)]
+    line = [(b, z ^ r) for r in (1, 2, 3)]
+    greet([sib] + flat + line)
+    f32, bf16 = jnp.float32, jnp.bfloat16
+    started = []
+
+    def go(src, dst, i, peer):
+        copy = remote(src, dst, sems, i, peer)
+        copy.start()
+        started.append(copy)
+        return copy
+
+    kv_c = [go(dkv_ref.at[(chip ^ r) * 2 + 1 - core], kv_sib.at[r], r, sib) for r in (3, 1, 2, 0)]
+    att_c = [go(datt_ref, att.at[r], 4 + r, line[r - 1]) for r in (3, 2, 1)]
+    nz_c = [go(gn_ref.at[pl.ds((z ^ r) * 8, 8)], nz_in.at[r - 1], 8 + r, line[r - 1]) for r in (1, 2, 3)]
+    kv_out = []
+    for k, r in enumerate((3, 1, 2, 0)):
+        kv_c[k].wait_recv()
+        both = dkv_ref[(chip ^ r) * 2 + core].astype(f32) + kv_sib[r].astype(f32)
+        kv_sum[r] = both.astype(bf16)
+        if r:
+            kv_out.append(go(kv_sum.at[r], kv_in.at[r - 1], 12 + r, flat[r - 1]))
+    ffn_c = [
+        go(gffn_ref.at[:, pl.ds(pl.multiple_of(((chip ^ r) * 2 + 1 - core) * 96, 96), 96)], ffn_sib.at[r], 16 + r, sib)
+        for r in (3, 1, 2, 0)
+    ]
+    ffn_out = []
+    for k, r in enumerate((3, 1, 2, 0)):
+        ffn_c[k].wait_recv()
+        mine = gffn_ref[:, pl.ds(pl.multiple_of(((chip ^ r) * 2 + core) * 96, 96), 96), :].astype(f32)
+        ffn_sum[r] = (mine + ffn_sib[r].astype(f32)).astype(bf16)
+        if r:
+            ffn_out.append(go(ffn_sum.at[r], ffn_in.at[r - 1], 20 + r, flat[r - 1]))
+    for c in nz_c:
+        c.wait_recv()
+    nrow[0] = gn_ref[pl.ds(z * 8, 8)] + nz_in[0] + nz_in[1] + nz_in[2]
+    np_c = [go(nrow.at[0], np_in.at[r], 24 + r, flat[r - 1]) for r in (1, 2, 3)]
+    for c in kv_out:
+        c.wait_recv()
+    dkvq[:, 0:384] = (
+        kv_sum[0].astype(f32) + kv_in[0].astype(f32) + kv_in[1].astype(f32) + kv_in[2].astype(f32)
+    ).astype(bf16)
+    dkvq[:, 384:640] = dq_ref[...]
+    dx_c = []
+    for r in (3, 2, 1, 0):
+        rows = pl.ds(pl.multiple_of((z ^ r) * 128, 128), 128)
+        got = dkvq[rows, :]
+        term = dot_nt(got[:, 0:512], w_ref[:, 0:512]) + dot_nt(got[:, 512:640], w_ref[:, 640:768])
+        if r:
+            part[r - 1] = term.astype(bf16)
+            dx_c.append(go(part.at[r - 1], part_in.at[r - 1], 28 + r, line[r - 1]))
+        else:
+            dx_ref[...] = done_ref[...] + term
+    for c in att_c:
+        c.wait_recv()
+    att[0] = datt_ref[...]
+    gat[:, 0:512] = dot_tn(tok_ref[...], dkvq[:, 0:512]).astype(bf16)
+    last = dot_tn(tok_ref[...], dkvq[:, 512:640])
+    outs = jnp.zeros((768, 256), f32)
+    for r in range(4):
+        outs = outs + dot_tn(att[r], mixed_ref[pl.ds(pl.multiple_of((z ^ r) * 128, 128), 128), :])
+    gat[:, 512:640] = outs[:, 0:128].astype(bf16)
+    gat[:, 640:768] = (outs[:, 128:256] + last).astype(bf16)
+    gat_c = [
+        go(gat.at[pl.ds(pl.multiple_of(((chip ^ r) * 2 + 1 - core) * 96, 96), 96)], gat_sib.at[r], 32 + r, sib)
+        for r in (3, 1, 2, 0)
+    ]
+    gat_out = []
+    for k, r in enumerate((3, 1, 2, 0)):
+        gat_c[k].wait_recv()
+        mine = gat[pl.ds(pl.multiple_of(((chip ^ r) * 2 + core) * 96, 96), 96), :].astype(f32)
+        gat_sum[r] = (mine + gat_sib[r].astype(f32)).astype(bf16)
+        if r:
+            gat_out.append(go(gat_sum.at[r], gat_in.at[r - 1], 36 + r, flat[r - 1]))
+    for c in np_c:
+        c.wait_recv()
+    nrow[1] = nrow[0] + np_in[1] + np_in[2] + np_in[3]
+    half = go(nrow.at[1], np_in.at[0], 24, sib)
+    for c in ffn_out:
+        c.wait_recv()
+    for t in range(3):
+        sffn_ref[t] = (
+            ffn_sum[0, t].astype(f32) + ffn_in[0, t].astype(f32) + ffn_in[1, t].astype(f32) + ffn_in[2, t].astype(f32)
+        )
+    for c in dx_c:
+        c.wait_recv()
+    dx_ref[...] += part_in[0].astype(f32) + part_in[1].astype(f32) + part_in[2].astype(f32)
+    half.wait_recv()
+    snorm_ref[...] = nrow[1] + np_in[0]
+    for c in gat_out:
+        c.wait_recv()
+    sattn_ref[...] = (
+        gat_sum[0].astype(f32) + gat_in[0].astype(f32) + gat_in[1].astype(f32) + gat_in[2].astype(f32)
+    )
+    for c in started:
+        c.wait_send()
+
+
+def run_finish(dkv, dq, toks, w, datt, mixed, done, gffn, gn):
+    f32, bf16 = jnp.float32, jnp.bfloat16
+    V = pltpu.VMEM
+    return pl.pallas_call(
+        finish,
+        out_shape=(
+            jax.ShapeDtypeStruct((128, 768), f32),
+            jax.ShapeDtypeStruct((96, 768), f32),
+            jax.ShapeDtypeStruct((3, 96, 768), f32),
+            jax.ShapeDtypeStruct((8, 768), f32),
+        ),
+        in_specs=[VM] * 9,
+        out_specs=(VM,) * 4,
+        scratch_shapes=[
+            V((4, 512, 384), bf16), V((4, 512, 384), bf16), V((3, 512, 384), bf16),
+            V((4, 3, 96, 768), bf16), V((4, 3, 96, 768), bf16), V((3, 3, 96, 768), bf16),
+            V((768, 768), bf16), V((4, 96, 768), bf16), V((4, 96, 768), bf16), V((3, 96, 768), bf16),
+            V((3, 128, 768), bf16), V((3, 128, 768), bf16), V((4, 128, 768), bf16), V((512, 640), bf16),
+            V((3, 8, 768), f32), V((2, 8, 768), f32), V((4, 8, 768), f32),
+            pltpu.SemaphoreType.DMA((2, 40)),
+        ],
+        compiler_params=pltpu.CompilerParams(
+            collective_id=5, has_side_effects=True, vmem_limit_bytes=56 << 20
+        ),
+        name="finish",
+    )(dkv, dq, toks, w, datt, mixed, done, gffn, gn)
+
+
+PACK = (1, 4, 2, 5, 7, 8, 0, 3)
+
+
+def packed(w_qkv, w_out):
+    piece = [w_qkv[:, 64 * i : 64 * i + 64] for i in range(9)]
+    out = w_out.T
+    return jnp.concatenate([piece[i] for i in PACK] + [out[:, :128], piece[6], out[:, 128:]], axis=1)
+
+
+def unpacked(g):
+    piece = [g[:, 64 * i : 64 * i + 64] for i in range(12)]
+    qkv = jnp.concatenate([piece[i] for i in (6, 0, 2, 7, 1, 3, 10, 4, 5)], axis=1)
+    return qkv, jnp.concatenate([piece[8], piece[9], piece[11]], axis=1).T
 
 
 def fast_shards(
@@ -494,20 +651,20 @@
     share = w_qkv.shape[0]
     bf16 = jnp.bfloat16
 
-    attn_w = lax.all_gather(jnp.concatenate([to_cols(w_qkv), w_out.T], axis=1), "blk", axis=0, tiled=True)
+    attn_w = lax.all_gather(packed(w_qkv, w_out), "blk", axis=0, tiled=True)
     ffn_w = lax.all_gather(
         jnp.concatenate([w_gate_up, w_down.T[None]], axis=0), "blk", axis=1, tiled=True
     )
     norms = lax.all_gather(norm_params.reshape(share), ("blk", "head"), axis=0, tiled=False)
     norms = norms.reshape(blk_n, heads_n, share).transpose(1, 0, 2).reshape(heads_n, width).astype(jnp.float32)
     group_tokens = lax.all_gather(tokens, "head", axis=0, tiled=True)
-    w_in = attn_w[:, :576]
-    out_t = attn_w[:, 576:]
+    out_pad = attn_w[:, 512:]
     w_gate, w_up, down_t = ffn_w[0], ffn_w[1], ffn_w[2]
 
-    kvq = jnp.dot(group_tokens, w_in, preferred_element_type=jnp.float32).astype(bf16)
+    kvq = jnp.dot(group_tokens, attn_w, preferred_element_type=jnp.float32).astype(bf16)
     kv = lax.all_gather(kvq[:, :384], "blk", axis=0, tiled=True).reshape(devs, tok_rows, 384)
-    q = (kvq[:, 384:] * bf16(HEAD_DIM ** (-0.5))).reshape(heads_n, tok_rows, 192)
+    q = jnp.concatenate([kvq[:, 384:512], kvq[:, 640:]], axis=1) * bf16(HEAD_DIM ** (-0.5))
+    q = q.reshape(heads_n, tok_rows, 256)
 
     seq_ends = prefix_sums(lengths)
     code = placement.astype(jnp.float32) + SEQ_STEP * seq_of(placement, seq_ends).astype(jnp.float32)
@@ -522,9 +679,8 @@
 
     mixed, lse = run_attend(span, slopes, q, kv, kcode, qcode)
     mixed_rows = mixed.reshape(group_rows, 256)
-    out_pad = pad_heads(out_t.T)
     attn_out = lax.psum_scatter(
-        jnp.dot(mixed_rows, out_pad, preferred_element_type=jnp.float32).astype(bf16),
+        dot_back(mixed_rows, out_pad).astype(bf16),
         "head", scatter_dimension=0, tiled=True,
     ).astype(jnp.float32)
     resid_one = tokens.astype(jnp.float32) + attn_out
@@ -550,34 +706,27 @@
     g_ffn = jnp.stack(
         [weight_grad(ffn_rows, d_gate_low), weight_grad(ffn_rows, d_up_low), weight_grad(branch_rows, gated_low)]
     ).astype(bf16)
-    s_ffn = lax.psum_scatter(g_ffn, "blk", scatter_dimension=1, tiled=True).astype(jnp.float32)
     d_one, d_gain_one, d_shift_one = norm_one_back(d_hidden)
     attn_rows = lax.all_gather(d_one.astype(bf16), "head", axis=0, tiled=True)
-    d_heads = dot_back(attn_rows, out_pad).astype(bf16)
+    d_heads = jnp.dot(attn_rows, out_pad, preferred_element_type=jnp.float32).astype(bf16)
     d_q, dkv = run_attend_back(
         span, slopes, q, kv, kcode, qcode, mixed, d_heads.reshape(heads_n, tok_rows, 256), lse
     )
-    d_kv = lax.psum_scatter(dkv.reshape(devs * tok_rows, 384), "blk", scatter_dimension=0, tiled=True)
-    d_kvq = jnp.concatenate([d_kv, d_q.reshape(group_rows, 192)], axis=1)
-    input_grad = d_one + lax.psum_scatter(
-        dot_back(d_kvq, w_in).astype(bf16), "head", scatter_dimension=0, tiled=True
-    ).astype(jnp.float32)
-    g_out_t = weight_grad(attn_rows, mixed_rows)
-    g_attn = jnp.concatenate(
-        [weight_grad(group_tokens, d_kvq), g_out_t[:, :128], g_out_t[:, 192:]], axis=1
-    ).astype(bf16)
-    s_attn = lax.psum_scatter(g_attn, "blk", scatter_dimension=0, tiled=True).astype(jnp.float32)
     g_norm = jnp.stack([d_gain_one, d_shift_one, d_gain_two, d_shift_two], axis=0)
-    g_norm = g_norm.reshape(heads_n, blk_n, share).transpose(1, 0, 2).reshape(devs, share)
-    s_norm = lax.psum_scatter(g_norm, ("blk", "head"), scatter_dimension=0, tiled=True)
+    g_norm = jnp.pad(g_norm[:, None, :], ((0, 0), (0, 7), (0, 0))).reshape(8 * heads_n, width)
+    input_grad, s_attn, s_ffn, s_norm = run_finish(
+        dkv.reshape(blk_n, group_rows, 384), d_q.reshape(group_rows, 256), group_tokens, attn_w,
+        d_one.astype(bf16), mixed_rows, d_one, g_ffn, g_norm,
+    )
+    s_qkv, s_out = unpacked(s_attn)
     return (
         result.astype(bf16),
         input_grad,
-        from_cols(s_attn[:, :576]),
-        s_attn[:, 576:].T,
+        s_qkv,
+        s_out,
         s_ffn[:2],
         s_ffn[2].T,
-        s_norm.reshape(share, 1),
+        lax.dynamic_slice(s_norm, (0, blk_idx * share), (1, share)).reshape(share, 1),
     )
 
 

time: 462 us -> 365 us (0.79)
  waiting for transfers between devices: 184 us -> 75.9 us
  Pallas kernels: 41 us -> 95.9 us
  blocking collectives: 156 us -> 116 us
    reduce_scatter x4 -> x1, waiting for transfers between devices: 66.8 us -> 0.01 us  [fast_shards(): lax.psum_scatter(dot_back(mixed_rows, out_pad).astype(bf16), 'head', scat...]
    pallas_call x0 -> x1, Pallas kernels: none -> 54.6 us  [run_finish(): pl.pallas_call(finish, out_shape=(jax.ShapeDtypeStruct((128, 768), f32),...]
    unnamed x2 -> x1, blocking collectives: 79.9 us -> 40.5 us
    unnamed x11 -> x6, waiting for transfers between devices: 37.9 us -> 0.1 us
    reduce_scatter x1, waiting for transfers between devices: 22.7 us -> 16.5 us  [fast_shards(): lax.psum_scatter(hidden_part.astype(bf16), 'head', scatter_dimension=0, t...]
  transfers between devices with their start and end apart: 10 -> 6, of which waited for: 8 -> 4; matrix products, arithmetic and copies ran while one was open for 6% -> 3% of each run, Pallas kernels for 0% -> 0%
where the time goes in v3:
time: 365 us; the launch traced here: 364 us
  blocking collectives  116 us (32%)
  Pallas kernels  95.9 us (26%)
  waiting for transfers between devices  75.9 us (21%)
  matrix products  28.4 us (8%)
  local copies, waits for them, and re-layouts  19.4 us (5%)
  between operations  14.6 us (4%)
  other arithmetic  13.2 us (4%)
    pallas_call x1, Pallas kernels, run_finish(): pl.pallas_call(finish, out_shape=(jax.ShapeDtypeStruct((128, 768), f32),...  54.6 us
    unnamed x1, blocking collectives  40.5 us
    all_gather x1, waiting for transfers between devices, fast_shards(): lax.all_gather(kvq[:, :384], 'blk', axis=0, tiled=True)  30.7 us
    pallas_call x1, Pallas kernels, run_attend_back(): pl.pallas_call(attend_back, out_shape=(jax.ShapeDtypeStruct((heads_n, slo...  26.1 us
    reduce_scatter x1, waiting for transfers between devices, fast_shards(): lax.psum_scatter(dot_back(gated_low, down_t).astype(bf16), 'head', scatte...  23.2 us
    all_gather x1, blocking collectives, fast_shards(): group_tokens = lax.all_gather(tokens, 'head', axis=0, tiled=True)  21.5 us
    all_gather x1, blocking collectives, fast_shards(): ffn_rows = lax.all_gather(hidden.astype(bf16), 'head', axis=0, tiled=True)  18.4 us
    all_gather x1, blocking collectives, fast_shards(): branch_rows = lax.all_gather(d_two.astype(bf16), 'head', axis=0, tiled=True)  18.2 us
  transfers between devices with their start and end apart: 6, of which 4 were waited for; matrix products, arithmetic and copies ran while one was open for 3% of the time, Pallas kernels for 0%

profile of v3, /device:TPU:0, one launch (start us, length us, event | category | flops | bytes accessed | tf_op | source)
XLA Modules:
  0.0 364.0 jit_solution(2427387516143394108)
XLA Ops:
  7.2 0.9 copy.47
  8.1 0.9 slice.113
  9.0 0.9 fusion.37
  10.0 0.8 concatenate.23
  10.8 21.5 %all_gather.25.tok_ref = bf16[512,768]{1,0:T(8,128)(2,1)S(1)} all-gather(bf16[128,768]{1,0:T(8,128)(2,1)} %param.10), channel_id=1, replica_groups=mesh['blk'=8,'head'=4] {'head'}, dimensions={0}, use_global_device_ids=true | all-gather | bytes 983040 | tf_op jit(solution)/shard_map/all_gather | solution.py:660
  32.3 5.3 %all-gather.5.cloned.1.call-done.w_ref = bf16[768,768]{1,0:T(8,128)(2,1)} async-done(((bf16[96,768]{1,0:T(8,128)(2,1)}), bf16[768,768]{1,0:T(8,128)(2,1)}) %all-gather.5.cloned.1.call-update) | async-done | bytes 1179664 | tf_op jit(solution)/shard_map/all_gather | solution.py:654
  37.7 2.0 fusion.9
  39.8 0.8 slice.146
  42.3 30.7 %all-gather.7.cloned.1.call-done = bf16[4096,384]{1,0:T(8,128)(2,1)} async-done(((bf16[512,384]{1,0:T(8,128)(2,1)}), bf16[4096,384]{1,0:T(8,128)(2,1)}) %all-gather.7.cloned.1.call-update) | async-done | bytes 3145744 | tf_op jit(solution)/shard_map/all_gather | solution.py:665
  73.7 1.9 copy-done
  75.6 15.2 %attend.1 = (bf16[4,128,256]{2,1,0:T(8,128)(2,1)S(1)}, f32[4,8,128]{2,1,0:T(8,128)S(1)}) custom-call(s32[4,2]{1,0:T(4,128)S(1)} %pad_add_fusion.span_ref, f32[3]{0:T(128)S(1)} %dynamic_slice.9.slope_ref, bf16[4,128,256]{2,1,0:T(8,128)(2,1)S(1)} %maximum_multiply_fusion.q_ref, bf16[32,128,384]{2,1,0:T(8,128)(2,1)S(1)} %bitcast.69, ...), custom_call_target="tpu_custom_call" | custom-call | tf_op jit(solution)/shard_map/attend/pallas_call | solution.py:419
  90.8 2.4 convolution_convert_fusion.5
  93.3 0.8 pad_maximum_fusion.1
  94.5 40.5 %all-reduce.1 = bf16[3072]{0:T(1024)(128)(2,1)S(1)} all-reduce(bf16[3072]{0:T(1024)(128)(2,1)S(1)} %dynamic-update-slice), channel_id=2, replica_groups=mesh['blk'=8,'head'=4] {'blk','head'}, use_global_device_ids=true, to_apply=%add.1 | all-reduce | flops 3072 | bytes 12288
  135.2 1.1 fusion.19
  136.3 1.1 multiply_reduce_fusion.3
  137.4 1.1 fusion.22
  138.5 18.4 %all_gather.28 = bf16[512,768]{1,0:T(8,128)(2,1)} all-gather(bf16[128,768]{1,0:T(8,128)(2,1)S(1)} %fusion.22), channel_id=1, replica_groups=mesh['blk'=8,'head'=4] {'head'}, dimensions={0}, use_global_device_ids=true | all-gather | bytes 983040 | tf_op jit(solution)/shard_map/all_gather | solution.py:688
  156.9 2.4 fusion.11
  159.3 6.8 %multiply_convert_fusion.1 = (bf16[512,768]{1,0:T(8,128)(2,1)S(1)}, f32[512,768]{1,0:T(8,128)}, f32[512,768]{1,0:T(8,128)}) fusion(f32[512,768]{1,0:T(8,128)S(1)} %fusion.11, bf16[512,768]{1,0:T(8,128)(2,1)S(1)} %copy-done.9, bf16[3,768,768]{2,1,0:T(8,128)(2,1)} %all-gather.9.cloned.1.call-done), kind=kOutput, calls=%fused_computation.6 | convolution fusion | flops 629932032 | bytes 7471104 | tf_op jit(solution)/shard_map/dot_general | solution.py:690
  166.2 0.9 copy-done.25
  167.0 3.0 convolution_convert_fusion.4
  170.3 23.2 %reduce-scatter.6.cloned.1.call-done = bf16[128,768]{1,0:T(8,128)(2,1)} async-done(((bf16[512,768]{1,0:T(8,128)(2,1)}), bf16[128,768]{1,0:T(8,128)(2,1)}) %reduce-scatter.6.cloned.1.call-update) | async-done | bytes 196624 | tf_op jit(solution)/shard_map/reduce_scatter | solution.py:693
  193.5 1.2 fusion.32
  195.1 2.1 fusion.31
  197.3 18.2 %all_gather.30 = bf16[512,768]{1,0:T(8,128)(2,1)S(1)} all-gather(bf16[128,768]{1,0:T(8,128)(2,1)S(1)} %add_convert_fusion.3), channel_id=1, replica_groups=mesh['blk'=8,'head'=4] {'head'}, dimensions={0}, use_global_device_ids=true | all-gather | bytes 983040 | tf_op jit(solution)/shard_map/all_gather | solution.py:698
  215.5 3.9 %multiply_convert_fusion = (bf16[512,768]{1,0:T(8,128)(2,1)S(1)}, bf16[512,768]{1,0:T(8,128)(2,1)S(1)}) fusion(f32[512,768]{1,0:T(8,128)} %get-tuple-element.65, f32[512,768]{1,0:T(8,128)} %copy-done.20, f32[512,768]{1,0:T(8,128)} %get-tuple-element.88, bf16[512,768]{1,0:T(8,128)(2,1)S(1)} %all_gather.30, bf16[3,768,768]{2,1,0:T(8,128)(2,1)S(1)} %copy-done.16), kind=kOutput, calls=%fused_computation.4 | convolution fusion | flops 611057664 | bytes 8257536 | tf_op jit(solution)/shard_map/dot_general | solution.py:699
  219.4 0.8 fusion.10
  220.6 1.7 add_convert_fusion
  222.3 2.3 fusion.8
  224.7 0.8 fusion.7
  225.8 0.8 fusion.6
  226.6 2.0 pad_maximum_fusion.gffn_ref
  228.6 16.5 %reduce-scatter.8.cloned.1.call-done = bf16[128,768]{1,0:T(8,128)(2,1)} async-done(((bf16[512,768]{1,0:T(8,128)(2,1)}), bf16[128,768]{1,0:T(8,128)(2,1)}) %reduce-scatter.8.cloned.1.call-update) | async-done | bytes 196624 | tf_op jit(solution)/shard_map/reduce_scatter | solution.py:703
  245.1 1.2 multiply_reduce_fusion.1
  247.3 0.9 fusion.30
  248.3 17.9 %all_gather.31 = bf16[512,768]{1,0:T(8,128)(2,1)S(1)} all-gather(bf16[128,768]{1,0:T(8,128)(2,1)S(1)} %get-tuple-element.56.datt_ref), channel_id=1, replica_groups=mesh['blk'=8,'head'=4] {'head'}, dimensions={0}, use_global_device_ids=true | all-gather | bytes 983040 | tf_op jit(solution)/shard_map/all_gather | solution.py:710
  266.2 1.4 convolution_convert_fusion.6
  267.6 26.1 %attend_back.1 = (bf16[4,128,256]{2,1,0:T(8,128)(2,1)S(1)}, bf16[32,128,384]{2,1,0:T(8,128)(2,1)}) custom-call(s32[4,2]{1,0:T(4,128)S(1)} %pad_add_fusion.span_ref, f32[3]{0:T(128)S(1)} %dynamic_slice.9.slope_ref, bf16[4,128,256]{2,1,0:T(8,128)(2,1)S(1)} %maximum_multiply_fusion.q_ref, bf16[32,128,384]{2,1,0:T(8,128)(2,1)} %bitcast.68, ...), custom_call_target="tpu_custom_call" | custom-call | tf_op jit(solution)/shard_map/attend_back/pallas_call | solution.py:436
  294.4 54.6 %finish.1 = (f32[128,768]{1,0:T(8,128)}, f32[96,768]{1,0:T(8,128)}, f32[3,96,768]{2,1,0:T(8,128)}, f32[8,768]{1,0:T(8,128)}) custom-call(bf16[8,512,384]{2,1,0:T(8,128)(2,1)} %bitcast.74, bf16[512,256]{1,0:T(8,128)(2,1)} %bitcast.72, bf16[512,768]{1,0:T(8,128)(2,1)} %copy-done.5, bf16[768,768]{1,0:T(8,128)(2,1)} %all-gather.5.cloned.1.call-done.w_ref, ...), custom_call_target="tpu_custom_call" | custom-call | tf_op jit(solution)/shard_map/finish/pallas_call | solution.py:600
  349.0 0.9 fusion.35
  349.9 1.1 fusion.36
  351.0 1.7 slice_bitcast_fusion.9
  352.7 0.9 slice.140
  353.6 0.7 copy.50
  354.4 1.3 dynamic-slice_bitcast_fusion
  355.6 0.8 concatenate.28
  356.4 0.7 copy.53
  (119 shorter events, 6.2 us)
Async XLA Ops:
  7.2 30.5 %all-gather.5.cloned.1.call-start = ((), (), s32[]{:S(2)}) async-start(), calls=%async_computation.3 | async-start | bytes 1327104 | tf_op jit(solution)/shard_map/all_gather | solution.py:654
  10.8 62.3 %all-gather.7.cloned.1.call-start = ((), (), s32[]{:S(2)}) async-start(), calls=%async_computation.4 | async-start | bytes 3538944 | tf_op jit(solution)/shard_map/all_gather | solution.py:665
  32.3 7.4 %copy-start.5 = (bf16[512,768]{1,0:T(8,128)(2,1)}, bf16[512,768]{1,0:T(8,128)(2,1)S(1)}, u32[]{:S(2)}) copy-start(bf16[512,768]{1,0:T(8,128)(2,1)S(1)} %all_gather.25.tok_ref) | copy-start | bytes 2359300
  32.3 8.3 %copy-start.17 = (s32[8]{0:T(128)S(1)}, s32[8]{0:T(128)}, u32[]{:S(2)}) copy-start(s32[8]{0:T(128)} %param.17) | copy-start | bytes 100
  32.3 9.1 %copy-start.15 = (s32[4096]{0:T(1024)S(1)}, s32[4096]{0:T(1024)}, u32[]{:S(2)}) copy-start(s32[4096]{0:T(1024)} %param.18) | copy-start | bytes 49156
  39.8 2.3 copy-start.18
  40.6 94.7 %reduce-scatter.4.cloned.1.call-start = ((), (), s32[]{:S(2)}) async-start(), calls=%async_computation.5 | async-start | bytes 983040 | tf_op jit(solution)/shard_map/reduce_scatter | solution.py:682
  73.7 1.9 copy-start
  90.8 176.8 %copy-start.1 = (bf16[4,128,256]{2,1,0:T(8,128)(2,1)}, bf16[4,128,256]{2,1,0:T(8,128)(2,1)S(1)}, u32[]{:S(2)}) copy-start(bf16[4,128,256]{2,1,0:T(8,128)(2,1)S(1)} %get-tuple-element.15.out_ref) | copy-start | bytes 786436
  90.8 2.5 copy-start.13
  90.8 2.5 copy-start.14
  90.8 3.4 copy-start.19
  90.8 44.4 %copy-start.3 = (bf16[128,768]{1,0:T(8,128)(2,1)S(1)}, bf16[128,768]{1,0:T(8,128)(2,1)}, u32[]{:S(2)}) copy-start(bf16[128,768]{1,0:T(8,128)(2,1)} %param.10) | copy-start | bytes 589828
  93.3 63.7 %all-gather.9.cloned.1.call-start = ((), (), s32[]{:S(2)}) async-start(), calls=%async_computation.6 | async-start | bytes 3981312 | tf_op jit(solution)/shard_map/all_gather | solution.py:655
  94.2 99.3 %reduce-scatter.6.cloned.1.call-start = ((), (), s32[]{:S(2)}) async-start(), calls=%async_computation.7 | async-start | bytes 983040 | tf_op jit(solution)/shard_map/reduce_scatter | solution.py:693
  156.9 2.4 copy-start.9
  159.3 6.9 %copy-start.20 = (f32[512,768]{1,0:T(8,128)}, f32[512,768]{1,0:T(8,128)S(1)}, u32[]{:S(2)}) copy-start(f32[512,768]{1,0:T(8,128)S(1)} %fusion.11) | copy-start | bytes 4718596
  166.2 0.9 copy-start.25
  167.0 26.5 %copy-start.4 = (bf16[128,768]{1,0:T(8,128)(2,1)S(1)}, bf16[128,768]{1,0:T(8,128)(2,1)}, u32[]{:S(2)}) copy-start(bf16[128,768]{1,0:T(8,128)(2,1)} %reduce-scatter.4.cloned.1.call-done) | copy-start | bytes 589828
  170.0 24.8 %copy-start.8 = (bf16[128,768]{1,0:T(8,128)(2,1)S(1)}, bf16[128,768]{1,0:T(8,128)(2,1)}, u32[]{:S(2)}) copy-start(bf16[128,768]{1,0:T(8,128)(2,1)} %param.19) | copy-start | bytes 589828
  170.1 75.0 %reduce-scatter.8.cloned.1.call-start = ((), (), s32[]{:S(2)}) async-start(), calls=%async_computation.8 | async-start | bytes 983040 | tf_op jit(solution)/shard_map/reduce_scatter | solution.py:703
  194.7 20.8 %copy-start.16 = (bf16[3,768,768]{2,1,0:T(8,128)(2,1)S(1)}, bf16[3,768,768]{2,1,0:T(8,128)(2,1)}, u32[]{:S(2)}) copy-start(bf16[3,768,768]{2,1,0:T(8,128)(2,1)} %all-gather.9.cloned.1.call-done) | copy-start | bytes 10616836
  215.5 3.9 %copy-start.11 = (bf16[512,768]{1,0:T(8,128)(2,1)}, bf16[512,768]{1,0:T(8,128)(2,1)S(1)}, u32[]{:S(2)}) copy-start(bf16[512,768]{1,0:T(8,128)(2,1)S(1)} %all_gather.30) | copy-start | bytes 2359300
  219.4 0.9 copy-start.23
  219.4 1.1 copy-start.21
  222.3 2.3 copy-start.10
  222.3 2.3 copy-start.22
  224.7 1.1 copy-start.24
  248.3 45.4 %copy-start.6 = (bf16[128,768]{1,0:T(8,128)(2,1)}, bf16[128,768]{1,0:T(8,128)(2,1)S(1)}, u32[]{:S(2)}) copy-start(bf16[128,768]{1,0:T(8,128)(2,1)S(1)} %get-tuple-element.56.datt_ref) | copy-start | bytes 589828
  293.7 0.7 copy-start.2
  349.0 3.8 %copy-start.7 = (f32[3,96,768]{2,1,0:T(8,128)S(1)}, f32[3,96,768]{2,1,0:T(8,128)}, u32[]{:S(2)}) copy-start(f32[3,96,768]{2,1,0:T(8,128)} %get-tuple-element.21) | copy-start | bytes 2654212
  351.0 5.5 %copy-start.12 = (f32[128,768]{1,0:T(8,128)S(1)}, f32[128,768]{1,0:T(8,128)}, u32[]{:S(2)}) copy-start(f32[128,768]{1,0:T(8,128)} %get-tuple-element.99) | copy-start | bytes 1179652
Sparse Core Ops, SparseCore 0:
  10.9 26.7 all-gather.4
  40.7 32.3 all-gather.6
  93.4 23.3 reduce-scatter.3
  119.2 34.0 all-gather.8
  170.2 23.2 reduce-scatter.5
  222.4 22.6 reduce-scatter.7
